TPU v7x, 512 devices: a whole 4x8x8 slice. The times are simulated.
512 devices in a mesh: dp: 16 (over y, core), expert: 32 (over x, z).
Axes of the slice: x: 4, y: 8, z: 8, core: 2. Of those that a mesh axis runs over, the one named last changes fastest.
Arguments:
- tokens: bfloat16 [65536, 2048], P(('dp', 'expert')), may hold values from -6 to 6
- cotangent: bfloat16 [65536, 2048], P(('dp', 'expert')), may hold values from -5 to 5
- routes: int32 [65536, 1], P(('dp', 'expert')), may hold values from 0 to 7; in each aligned block of 128 rows (0 to 127, 128 to 255, ...) at most 18 rows name the same one
- expert_gates: float32 [65536, 1], P(('dp', 'expert')), may hold values from 0.1 to 1
- gate_proj: bfloat16 [2048, 6144], P(None, 'expert'), may hold values from -0.125 to 0.125
- up_proj: bfloat16 [2048, 6144], P(None, 'expert'), may hold values from -0.125 to 0.125
- down_proj: bfloat16 [6144, 2048], P('expert'), may hold values from -0.21875 to 0.21875
Outputs:
- grad_input: bfloat16 [65536, 2048], P(('dp', 'expert'))
- grad_gate: float32 [2048, 6144], P('dp', 'expert')
- grad_up: float32 [2048, 6144], P('dp', 'expert')
- grad_down: float32 [6144, 2048], P('expert', 'dp')
Inputs may be any that keep to these rules, and one draw needn't show every extreme that they name: `routes`: each row names exactly one expert. Among the rows of one device no expert is named more than 18 times.
All inputs are finite; a program needn't handle non-finite values.
Results may differ from a plain program's by a relative error of at most 0.022.
Values may be sent and summed in bfloat16 or wider, within the bound.
A program may use at most 64 MiB of HBM per device.

v0:
```python
import jax
import jax.numpy as jnp
from jax import lax
from jax.sharding import PartitionSpec as P

EXPERTS = 8
MOST = 18


def build_slots(routes, capacity):
    flat_routes = routes.reshape(-1)
    one_hot = (flat_routes[:, None] == jnp.arange(EXPERTS, dtype=jnp.int32)[None, :]).astype(
        jnp.int32
    )
    before = jnp.cumsum(one_hot, axis=0) - one_hot
    position = jnp.sum(before * one_hot, axis=1)
    return flat_routes * capacity + position


def body(tokens, cotangent, routes, expert_gates, gate_proj, up_proj, down_proj):
    tok_dev, model_dim = tokens.shape
    top_k = routes.shape[1]
    expert_devs = lax.axis_size("expert")
    group_size = expert_devs // EXPERTS
    capacity = MOST
    slot_total = EXPERTS * capacity
    slot_of = build_slots(routes, capacity)
    owners = jnp.arange(tok_dev * top_k, dtype=jnp.int32) // top_k
    slot_table = jnp.full((slot_total,), tok_dev, jnp.int32).at[slot_of].set(owners)
    slot_gate = jnp.zeros((slot_total,), jnp.float32).at[slot_of].set(expert_gates.reshape(-1))
    x_slots = jnp.take(tokens, slot_table, axis=0, mode="fill", fill_value=0)
    dy_slots = (
        jnp.take(cotangent, slot_table, axis=0, mode="fill", fill_value=0).astype(jnp.float32)
        * slot_gate[:, None]
    ).astype(jnp.bfloat16)

    def copies(values):
        spread = values.reshape(EXPERTS, 1, capacity, model_dim)
        return jnp.broadcast_to(spread, (EXPERTS, group_size, capacity, model_dim)).reshape(
            expert_devs, capacity, model_dim
        )

    x_recv, dy_recv = (
        lax.all_to_all(copies(x_slots), "expert", split_axis=0, concat_axis=0, tiled=True),
        lax.all_to_all(copies(dy_slots), "expert", split_axis=0, concat_axis=0, tiled=True),
    )
    in_rows = x_recv.reshape(expert_devs * capacity, model_dim)
    scaled = dy_recv.reshape(expert_devs * capacity, model_dim)
    pre_gate = jnp.dot(in_rows, gate_proj, preferred_element_type=jnp.float32)
    pre_up = jnp.dot(in_rows, up_proj, preferred_element_type=jnp.float32)
    gate_sig = jax.nn.sigmoid(pre_gate)
    hidden = (pre_gate * gate_sig * pre_up).astype(jnp.bfloat16)
    by_width = (((1,), (1,)), ((), ()))
    by_rows = (((0,), (0,)), ((), ()))
    d_hidden = lax.dot_general(scaled, down_proj, by_width, preferred_element_type=jnp.float32)
    d_gate = (d_hidden * pre_up * gate_sig * (1.0 + pre_gate * (1.0 - gate_sig))).astype(
        jnp.bfloat16
    )
    d_up = (d_hidden * pre_gate * gate_sig).astype(jnp.bfloat16)
    grad_down = lax.dot_general(hidden, scaled, by_rows, preferred_element_type=jnp.float32)
    grad_gate = lax.dot_general(in_rows, d_gate, by_rows, preferred_element_type=jnp.float32)
    grad_up = lax.dot_general(in_rows, d_up, by_rows, preferred_element_type=jnp.float32)
    grad_gate, grad_up, grad_down = (
        lax.psum_scatter(
            grad_gate.astype(jnp.bfloat16), "dp", scatter_dimension=0, tiled=True
        ).astype(jnp.float32),
        lax.psum_scatter(
            grad_up.astype(jnp.bfloat16), "dp", scatter_dimension=0, tiled=True
        ).astype(jnp.float32),
        lax.psum_scatter(
            grad_down.astype(jnp.bfloat16), "dp", scatter_dimension=1, tiled=True
        ).astype(jnp.float32),
    )
    joined_grads = jnp.concatenate([d_gate, d_up], 1)
    joined_proj = jnp.concatenate([gate_proj, up_proj], 1)
    partial_value = lax.dot_general(
        joined_grads, joined_proj, by_width, preferred_element_type=jnp.float32
    ).astype(jnp.bfloat16)
    returned = lax.all_to_all(
        partial_value.reshape(expert_devs, capacity, model_dim),
        "expert",
        split_axis=0,
        concat_axis=0,
        tiled=True,
    )
    summed = jnp.sum(
        returned.reshape(EXPERTS, group_size, capacity, model_dim).astype(jnp.float32), axis=1
    )
    summed = summed.reshape(slot_total, model_dim)
    grad_input = jnp.take(summed, slot_of, axis=0).reshape(tok_dev, top_k, model_dim).sum(axis=1)
    return (grad_input.astype(jnp.bfloat16), grad_gate, grad_up, grad_down)


def solution(mesh):
    in_specs = (
        P(("dp", "expert"), None),
        P(("dp", "expert"), None),
        P(("dp", "expert"), None),
        P(("dp", "expert"), None),
        P(None, "expert"),
        P(None, "expert"),
        P("expert", None),
    )
    out_specs = (P(("dp", "expert"), None), P("dp", "expert"), P("dp", "expert"), P("expert", "dp"))
    return jax.shard_map(body, mesh=mesh, in_specs=in_specs, out_specs=out_specs, check_vma=False)
```

profile of v0, /device:TPU:1, one launch (start us, length us, event | category | flops | bytes accessed | tf_op | source)
XLA Modules:
  0.0 393.3 jit_solution(6687252567635863338)
XLA Ops:
  7.2 0.0 copy-start
  7.2 0.8 fusion.7
  8.0 0.2 reduce_window_sum.11
  8.2 0.8 select_reduce_fusion
  9.0 0.7 and_bitcast_fusion
  9.7 1.0 scatter_custom_fusion
  10.7 1.1 scatter_custom_fusion.1
  11.8 2.7 gather_fusion.1
  14.5 0.3 multiply_convert_fusion
  14.8 0.2 broadcast_in_dim.49
  15.0 2.1 broadcast_in_dim.50
  17.1 0.0 copy-start.1
  17.1 14.0 %all-to-all-start = ((bf16[32,18,2048]{2,1,0:T(8,128)(2,1)}), bf16[32,18,2048]{2,1,0:T(8,128)(2,1)}, u32[]{:S(2)}, u32[]{:S(2)}) async-start(bf16[32,18,2048]{2,1,0:T(8,128)(2,1)} %bitcast.32), calls=%async_computation | async-start | bytes 6291456 | tf_op jit(solution)/shard_map/all_to_all | solution.py:45
  31.1 0.0 copy-done.1
  31.1 1.0 gather_fusion.2
  32.1 0.1 broadcast_select_fusion
  32.2 0.2 broadcast_in_dim.51
  32.4 70.2 %all-to-all-done = bf16[32,18,2048]{2,1,0:T(8,128)(2,1)} async-done(((bf16[32,18,2048]{2,1,0:T(8,128)(2,1)}), bf16[32,18,2048]{2,1,0:T(8,128)(2,1)}, u32[]{:S(2)}, u32[]{:S(2)}) %all-to-all-start) | async-done | bytes 2359328 | tf_op jit(solution)/shard_map/all_to_all | solution.py:45
  102.6 2.1 broadcast_in_dim.52
  104.7 8.9 %all-to-all-start.1 = ((bf16[32,18,2048]{2,1,0:T(8,128)(2,1)}), bf16[32,18,2048]{2,1,0:T(8,128)(2,1)}, u32[]{:S(2)}, u32[]{:S(2)}) async-start(bf16[32,18,2048]{2,1,0:T(8,128)(2,1)} %bitcast.33), calls=%async_computation.1 | async-start | bytes 6291456 | tf_op jit(solution)/shard_map/all_to_all | solution.py:44
  113.6 0.0 reduce-scatter.14.cloned.1.call-start
  113.6 2.9 reshape.60
  116.6 0.0 copy-done
  116.6 0.0 copy-start.2
  116.6 1.8 fusion.14
  118.4 0.0 copy-done.2
  118.4 66.2 %all-to-all-done.1 = bf16[32,18,2048]{2,1,0:T(8,128)(2,1)} async-done(((bf16[32,18,2048]{2,1,0:T(8,128)(2,1)}), bf16[32,18,2048]{2,1,0:T(8,128)(2,1)}, u32[]{:S(2)}, u32[]{:S(2)}) %all-to-all-start.1) | async-done | bytes 2359328 | tf_op jit(solution)/shard_map/all_to_all | solution.py:44
  184.6 2.9 reshape.62
  187.5 0.0 copy-start.4
  187.5 0.0 copy-start.5
  187.6 2.2 fusion.15
  189.8 0.0 copy-done.4
  189.8 0.0 copy-done.5
  189.8 0.0 copy-start.3
  189.8 1.8 multiply_convert_fusion.3
  191.7 0.0 copy-done.3
  191.7 1.7 convolution_convert_fusion.3
  193.4 2.2 copy.15
  195.6 0.0 reduce-scatter.14.cloned.1.call-update
  195.6 4.4 %convolution_convert_fusion = bf16[576,2048]{1,0:T(8,128)(2,1)} fusion(bf16[2048,192]{0,1:T(8,128)(2,1)} %param.14, bf16[2048,192]{0,1:T(8,128)(2,1)} %param.13, bf16[576,192]{0,1:T(8,128)(2,1)} %get-tuple-element.8, bf16[576,192]{0,1:T(8,128)(2,1)S(1)} %get-tuple-element.7), kind=kOutput, calls=%fused_computation.6 | convolution fusion | flops 911179776 | bytes 4374528 | tf_op jit(solution)/shard_map/dot_general | solution.py:76
  200.0 4.3 %reshape.63 = bf16[32,18,2048]{2,1,0:T(8,128)(2,1)} reshape(bf16[576,2048]{1,0:T(8,128)(2,1)} %convolution_convert_fusion) | data formatting | bytes 4718592 | tf_op jit(solution)/shard_map/reshape | solution.py:80
  204.3 9.3 %all-to-all-start.2 = ((bf16[32,18,2048]{2,1,0:T(8,128)(2,1)}), bf16[32,18,2048]{2,1,0:T(8,128)(2,1)}, u32[]{:S(2)}, u32[]{:S(2)}) async-start(bf16[32,18,2048]{2,1,0:T(8,128)(2,1)} %reshape.63), calls=%async_computation.2 | async-start | bytes 6291456 | tf_op jit(solution)/shard_map/all_to_all | solution.py:79
  213.6 0.0 reduce-scatter.12.cloned.1.call-start
  213.6 2.7 convolution_convert_fusion.1
  216.3 2.2 copy.13
  218.6 0.0 reduce-scatter.12.cloned.1.call-update
  218.6 0.2 reduce-scatter.10.cloned.1.call-start
  218.8 1.7 convolution_convert_fusion.2
  220.5 2.3 copy.11
  222.8 0.0 reduce-scatter.10.cloned.1.call-update
  222.8 33.9 %reduce-scatter.14.cloned.1.call-done = bf16[128,192]{1,0:T(8,128)(2,1)} async-done(((bf16[2048,192]{1,0:T(8,128)(2,1)}), bf16[128,192]{1,0:T(8,128)(2,1)}) %reduce-scatter.14.cloned.1.call-update) | async-done | bytes 49168
  256.7 0.9 copy.16
  257.7 0.7 convert_element_type.63
  258.4 60.9 %reduce-scatter.12.cloned.1.call-done = bf16[128,192]{1,0:T(8,128)(2,1)} async-done(((bf16[2048,192]{1,0:T(8,128)(2,1)}), bf16[128,192]{1,0:T(8,128)(2,1)}) %reduce-scatter.12.cloned.1.call-update) | async-done | bytes 49168
  319.3 0.9 copy.14
  320.2 0.7 convert_element_type.60
  320.9 59.7 %reduce-scatter.10.cloned.1.call-done = bf16[128,192]{1,0:T(8,128)(2,1)} async-done(((bf16[2048,192]{1,0:T(8,128)(2,1)}), bf16[128,192]{1,0:T(8,128)(2,1)}) %reduce-scatter.10.cloned.1.call-update) | async-done | bytes 49168
  380.5 0.9 copy.12
  381.5 0.7 convert_element_type.58
  382.2 0.0 all-to-all-done.2
  382.2 2.5 convert_reduce_fusion
  384.6 0.2 reshape.64
  384.8 0.9 gather_fusion
  385.8 1.0 select_convert_fusion
  (5 shorter events, 0.0 us)
Async XLA Ops:
  7.2 109.4 %copy-start = (bf16[192,2048]{1,0:T(8,128)(2,1)S(1)}, bf16[192,2048]{1,0:T(8,128)(2,1)}, u32[]{:S(2)}) copy-start(bf16[192,2048]{1,0:T(8,128)(2,1)} %param.15) | copy-start | bytes 2359300
  17.1 14.0 %copy-start.1 = (bf16[128,2048]{1,0:T(8,128)(2,1)S(1)}, bf16[128,2048]{1,0:T(8,128)(2,1)}, u32[]{:S(2)}) copy-start(bf16[128,2048]{1,0:T(8,128)(2,1)} %param.9) | copy-start | bytes 1572868
  17.1 85.5 %all-to-all-start = ((bf16[32,18,2048]{2,1,0:T(8,128)(2,1)}), bf16[32,18,2048]{2,1,0:T(8,128)(2,1)}, u32[]{:S(2)}, u32[]{:S(2)}) async-start(bf16[32,18,2048]{2,1,0:T(8,128)(2,1)} %bitcast.32), calls=%async_computation | async-start | bytes 6291456 | tf_op jit(solution)/shard_map/all_to_all | solution.py:45
  104.7 79.9 %all-to-all-start.1 = ((bf16[32,18,2048]{2,1,0:T(8,128)(2,1)}), bf16[32,18,2048]{2,1,0:T(8,128)(2,1)}, u32[]{:S(2)}, u32[]{:S(2)}) async-start(bf16[32,18,2048]{2,1,0:T(8,128)(2,1)} %bitcast.33), calls=%async_computation.1 | async-start | bytes 6291456 | tf_op jit(solution)/shard_map/all_to_all | solution.py:44
  113.6 143.2 %reduce-scatter.14.cloned.1.call-start = ((), (), s32[]{:S(2)}) async-start(), calls=%async_computation.8 | async-start | bytes 1114112
  116.6 1.8 copy-start.2
  187.5 2.3 copy-start.4
  187.5 2.3 copy-start.5
  189.8 1.9 copy-start.3
  204.3 177.9 %all-to-all-start.2 = ((bf16[32,18,2048]{2,1,0:T(8,128)(2,1)}), bf16[32,18,2048]{2,1,0:T(8,128)(2,1)}, u32[]{:S(2)}, u32[]{:S(2)}) async-start(bf16[32,18,2048]{2,1,0:T(8,128)(2,1)} %reshape.63), calls=%async_computation.2 | async-start | bytes 6291456 | tf_op jit(solution)/shard_map/all_to_all | solution.py:79
  213.6 105.7 %reduce-scatter.12.cloned.1.call-start = ((), (), s32[]{:S(2)}) async-start(), calls=%async_computation.7 | async-start | bytes 1114112
  218.6 162.0 %reduce-scatter.10.cloned.1.call-start = ((), (), s32[]{:S(2)}) async-start(), calls=%async_computation.6 | async-start | bytes 1114112
Sparse Core Ops, SparseCore 0:
  195.8 60.9 reduce-scatter.13
  259.8 59.4 reduce-scatter.11
  322.1 58.4 reduce-scatter.9
where the time goes:
time: 395 us; the launch traced here: 393 us
  waiting for transfers between devices  291 us (74%)
  starting transfers between devices  32.5 us (8%)
  local copies, waits for them, and re-layouts  31.1 us (8%)
  matrix products  16.3 us (4%)
  between operations  14 us (4%)
  other arithmetic  8.37 us (2%)
    unnamed x6, waiting for transfers between devices  155 us
    all_to_all x1, waiting for transfers between devices, body(): lax.all_to_all(copies(dy_slots), 'expert', split_axis=0, concat_axis=0, t...  70.2 us
    all_to_all x1, waiting for transfers between devices, body(): lax.all_to_all(copies(x_slots), 'expert', split_axis=0, concat_axis=0, ti...  66.2 us
    all_to_all x1, starting transfers between devices, body(): lax.all_to_all(copies(dy_slots), 'expert', split_axis=0, concat_axis=0, t...  14 us
    unnamed x18, local copies, waits for them, and re-layouts  9.6 us
    all_to_all x1, starting transfers between devices, body(): lax.all_to_all(partial_value.reshape(expert_devs, capacity, model_dim), '...  9.32 us
    all_to_all x1, starting transfers between devices, body(): lax.all_to_all(copies(x_slots), 'expert', split_axis=0, concat_axis=0, ti...  8.92 us
  transfers between devices with their start and end apart: 6, of which 5 were waited for; matrix products, arithmetic and copies ran while one was open for 7% of the time, Pallas kernels for 0%

commit v1 on v0

v1 whole, which is shorter than its diff:
```python
import jax
import jax.numpy as jnp
from jax import lax
from jax.experimental import pallas as pl
from jax.experimental.pallas import tpu as pltpu
from jax.sharding import PartitionSpec as P

MESH = pl.DeviceIdType.MESH
EXPERTS = 8
MOST = 18
TOK = 128
D = 2048
NX, NY, NZ = 4, 8, 8
HALF_HID = 96
WROWS = 3 * HALF_HID
GU = 2 * HALF_HID
BLK = D // NY
ROWS = EXPERTS * MOST
SEND = 48
BACK = 32
F32 = jnp.float32
BF16 = jnp.bfloat16
NT = (((1,), (1,)), ((), ()))
TN = (((0,), (0,)), ((), ()))
NN = (((1,), (0,)), ((), ()))


def dot(a, b, dims=NN):
    return lax.dot_general(a, b, dims, preferred_element_type=F32)


def iota(shape, dim):
    return lax.broadcasted_iota(jnp.int32, shape, dim)


def pick(cond):
    return jnp.where(cond, 1.0, 0.0).astype(BF16)


def kernel(
    routes, gates, tok, cot, gp, up, dn, gin, grads,
    xd, wall, rcv, xs, ds, gr, rb, tot, zb, dxp, dxr, ret, dgu,
    disp_s, disp_r, loc, sib_s, sib_r, wz_s, wz_r, ag_s, ag_r,
    dx_s, dx_r, ret_s, ret_r, rs_s, rs_r, zs_s, zs_r,
):
    di, ei = lax.axis_index("dp"), lax.axis_index("expert")
    y, c = di // 2, di % 2
    x, z = ei // NZ, ei % NZ
    h, zl = z // 4, z % 4
    sibling = {"dp": y * 2 + (1 - c), "expert": ei}
    above = {"dp": ((y + 1) % NY) * 2 + c, "expert": ei}
    below = {"dp": ((y + NY - 1) % NY) * 2 + c, "expert": ei}

    def at_x(dx, rel):
        return ((x + dx) % NX) * NZ + (z if rel == 0 else NZ - 1 - z)

    def at_z(q, core=None):
        dp = di if core is None else y * 2 + core
        return {"dp": dp, "expert": x * NZ + h * 4 + (zl + q) % 4}

    far = [(dx, rel) for rel in (0, 1) for dx in range(NX) if dx or rel]

    def remote(src, dst, send, recv, where):
        return pltpu.make_async_remote_copy(
            src_ref=src, dst_ref=dst, send_sem=send, recv_sem=recv,
            device_id=where, device_id_type=MESH,
        )

    barrier = pltpu.get_barrier_semaphore()
    partners = [sibling, above, below]
    partners += [{"dp": di, "expert": at_x(dx, rel)} for dx, rel in far]
    partners += [at_z(q, core) for q in (1, 2, 3) for core in (0, 1)]
    for p in partners:
        pl.semaphore_signal(barrier, inc=1, device_id=p, device_id_type=MESH)

    mine = pick(iota((HALF_HID, GU), 1) == iota((HALF_HID, GU), 0) + c * HALF_HID)

    def own_block(b):
        at = pl.multiple_of(b * BLK, BLK)
        wall[0, b, 0:HALF_HID, :] = dot(mine, gp[pl.ds(at, BLK), :], NT).astype(BF16)
        wall[0, b, HALF_HID:GU, :] = dot(mine, up[pl.ds(at, BLK), :], NT).astype(BF16)
        wall[0, b, GU:WROWS, :] = dot(mine, dn[:, pl.ds(at, BLK)]).astype(BF16)

    own_block(y)
    pl.semaphore_wait(barrier, len(partners))

    wz = [
        remote(wall.at[0, y], wall.at[q, y], wz_s.at[q - 1], wz_r.at[q - 1], at_z(q))
        for q in (1, 2, 3)
    ]
    for w in wz:
        w.start()

    route = routes[...]
    one_hot = pick(iota((TOK, 128), 1) == route)
    earlier = pick(iota((TOK, TOK), 0) > iota((TOK, TOK), 1))
    rank = jnp.sum(dot(earlier, one_hot) * one_hot.astype(F32), axis=1, keepdims=True)
    rank = rank.astype(jnp.int32)
    lanes = iota((TOK, EXPERTS * SEND), 1)
    first = route * SEND + rank
    place = jnp.concatenate([pick(lanes == first), pick(lanes == first + 24)], axis=0)
    weight = gates[...]
    for b in range(4):
        cols = slice(b * 512, b * 512 + 512)
        scaled = (cot[:, cols].astype(F32) * weight).astype(BF16)
        both = jnp.concatenate([tok[:, cols], scaled], axis=0)
        xd[:, cols] = dot(place, both, TN).astype(BF16)

    def rows_of(e, n):
        return pl.ds(pl.multiple_of(e * n, n), n)

    sends = []
    for i, (dx, rel) in enumerate(far):
        e = ((x + dx) % NX) * 2 + (h if rel == 0 else 1 - h)
        sends.append(
            remote(
                xd.at[rows_of(e, SEND)], rcv.at[c, rows_of(x * 2 + rel, SEND)],
                disp_s.at[i], disp_r.at[i], {"dp": di, "expert": at_x(dx, rel)},
            )
        )
        sends[-1].start()
    keep = pltpu.make_async_copy(
        xd.at[rows_of(x * 2 + h, SEND)], rcv.at[c, rows_of(x * 2, SEND)], loc
    )
    keep.start()

    def ag(way, t, q):
        b = (y - t + NY) % NY if way == 0 else (y + t) % NY
        ref = wall.at[q, b]
        if t == 3:
            ref = wall.at[q, b, pl.ds(way * (WROWS // 2), WROWS // 2)]
        return remote(
            ref, ref, ag_s.at[way, t, q - 1], ag_r.at[way, t, q - 1],
            above if way == 0 else below,
        )

    def ag_in(way, t, q):
        b = (y - 1 - t + NY) % NY if way == 0 else (y + 1 + t) % NY
        ref = wall.at[q, b]
        if t == 3:
            ref = wall.at[q, b, pl.ds(way * (WROWS // 2), WROWS // 2)]
        remote(
            ref, ref, ag_s.at[way, t, q - 1], ag_r.at[way, t, q - 1],
            above if way == 0 else below,
        ).wait_recv()

    for q in (1, 2, 3):
        wz[q - 1].wait_recv()
        for way in (0, 1):
            ag(way, 0, q).start()
    for k in range(1, NY):
        own_block((y + k) % NY)

    for t in (1, 2):
        for q in (1, 2, 3):
            for way in (0, 1):
                ag_in(way, t - 1, q)
                ag(way, t, q).start()

    def to_sibling(i, dx, rel):
        ref = rcv.at[c, rows_of(((x - dx + NX) % NX) * 2 + rel, SEND)]
        return remote(ref, ref, sib_s.at[i], sib_r.at[i], sibling)

    def from_sibling(i, dx, rel):
        ref = rcv.at[1 - c, rows_of(((x - dx + NX) % NX) * 2 + rel, SEND)]
        return remote(ref, ref, sib_s.at[i], sib_r.at[i], sibling)

    keep.wait()
    to_sibling(7, 0, 0).start()
    for i, (dx, rel) in enumerate(far):
        sends[i].wait_recv()
        to_sibling(i, dx, rel).start()

    for q in (1, 2, 3):
        for way in (0, 1):
            ag_in(way, 2, q)
            ag(way, 3, q).start()

    for i, (dx, rel) in enumerate(far + [(0, 0)]):
        from_sibling(i, dx, rel).wait_recv()

    row = iota((ROWS, EXPERTS * SEND), 0)
    for m in range(1, EXPERTS):
        row = row + jnp.where(iota((ROWS, EXPERTS * SEND), 0) >= MOST * m, SEND - MOST, 0)
    col = iota((ROWS, EXPERTS * SEND), 1)
    sel_x, sel_d = pick(col == row), pick(col == row + 24)
    for core in (0, 1):
        for b in range(4):
            cols = slice(b * 512, b * 512 + 512)
            part = rcv[core, :, cols]
            xs[core * ROWS:core * ROWS + ROWS, cols] = dot(sel_x, part).astype(BF16)
            ds[core * ROWS:core * ROWS + ROWS, cols] = dot(sel_d, part).astype(BF16)

    def rs(way, t, s):
        if t == 0:
            half = pl.ds(way * (WROWS // 2), WROWS // 2)
            src, dst = gr.at[s, (y + 4) % NY, half], rb.at[way, 0, s, half]
        else:
            src, dst = rb.at[way, t - 1, s], rb.at[way, t, s]
        return remote(
            src, dst, rs_s.at[way, t, s], rs_r.at[way, t, s],
            above if way == 0 else below,
        )

    def compute(s):
        pre = jnp.zeros((GU, 2 * ROWS), F32)
        dh = jnp.zeros((HALF_HID, 2 * ROWS), F32)
        for b in range(NY):
            cols = slice(b * BLK, b * BLK + BLK)
            pre = pre + dot(wall[s, b, 0:GU, :], xs[:, cols], NT)
            dh = dh + dot(wall[s, b, GU:WROWS, :], ds[:, cols], NT)
        g, u = pre[0:HALF_HID], pre[HALF_HID:GU]
        sig = 1.0 / (1.0 + jnp.exp(-g))
        hid = (g * sig * u).astype(BF16)
        d_gate = (dh * u * sig * (1.0 + g * (1.0 - sig))).astype(BF16)
        d_up = (dh * g * sig).astype(BF16)
        dboth = jnp.concatenate([d_gate, d_up], axis=0)
        dgu[s * GU:s * GU + GU, :] = dboth
        for k in range(NY):
            b = k
            cols = slice(b * BLK, b * BLK + BLK)
            gr[s, b, 0:GU, :] = dot(dboth, xs[:, cols]).astype(BF16)
            gr[s, b, GU:WROWS, :] = dot(hid, ds[:, cols]).astype(BF16)

    for s in range(4):
        if s:
            for way in (0, 1):
                ag_in(way, 3, s)
        compute(s)
        for way in (0, 1):
            rs(way, 0, s).start()

    j, i_ = iota((EXPERTS * BACK, ROWS), 0), iota((EXPERTS * BACK, ROWS), 1)
    spread = pick((i_ == j - (BACK - MOST) * (j // BACK)) & (j % BACK < MOST))
    for b in range(NY):
        cols = slice(b * BLK, b * BLK + BLK)
        rhs = jnp.concatenate([wall[s, b, 0:GU, :] for s in range(4)], axis=0)
        dx = dot(dgu[...], rhs, TN).astype(BF16)
        for core in (0, 1):
            dxp[core, :, cols] = dot(spread, dx[core * ROWS:core * ROWS + ROWS]).astype(BF16)
    dx_out = remote(dxp.at[1 - c], dxr, dx_s, dx_r, sibling)
    dx_out.start()

    def rs_add(way, t, s):
        rs(way, t, s).wait_recv()
        b = (y + 3 - t) % NY if way == 0 else (y - 3 + t + NY) % NY
        if t == 0:
            lo, hi = way * (WROWS // 2), (1 - way) * (WROWS // 2)
            a, o = pl.ds(lo, WROWS // 2), pl.ds(hi, WROWS // 2)
            rb[way, 0, s, a, :] = (rb[way, 0, s, a, :].astype(F32) + gr[s, b, a, :].astype(F32)).astype(BF16)
            rb[way, 0, s, o, :] = gr[s, b, o, :]
        else:
            rb[way, t, s] = (rb[way, t, s].astype(F32) + gr[s, b].astype(F32)).astype(BF16)

    for t in (0, 1, 2):
        for s in range(4):
            for way in (0, 1):
                rs_add(way, t, s)
                rs(way, t + 1, s).start()
        if t == 0:
            dx_out.wait_recv()
            dxr[...] = (dxr[...].astype(F32) + dxp[c].astype(F32)).astype(BF16)
            backs = []
            for i, (dx, rel) in enumerate(far):
                slot = ((x + dx) % NX) * 2 + rel
                backs.append(
                    remote(
                        dxr.at[rows_of(slot, BACK)], ret.at[rows_of(x * 2 + h, BACK)],
                        ret_s.at[i], ret_r.at[i], {"dp": di, "expert": at_x(dx, rel)},
                    )
                )
                backs[-1].start()
            back_own = pltpu.make_async_copy(
                dxr.at[rows_of(x * 2, BACK)], ret.at[rows_of(x * 2 + h, BACK)], loc
            )
            back_own.start()

    finals = []
    for s in range(4):
        for way in (0, 1):
            rs(way, 3, s).wait_recv()
        total = gr[s, y].astype(F32) + rb[0, 3, s].astype(F32) + rb[1, 3, s].astype(F32)
        for core in (0, 1):
            tot[s, core] = total[:, core * 128:core * 128 + 128].astype(BF16)
        if s:
            for core in (0, 1):
                k = 2 * s - 1 + core
                finals.append(
                    remote(tot.at[s, core], zb.at[s, c], zs_s.at[k], zs_r.at[s, c], at_z(4 - s, core))
                )
                finals[-1].start()
        else:
            finals.append(remote(tot.at[0, 1 - c], zb.at[0, c], zs_s.at[0], zs_r.at[0, c], sibling))
            finals[-1].start()
            zb[0, c] = tot[0, c]

    back_own.wait()
    for b in backs:
        b.wait_recv()
    take = pick(iota((TOK, EXPERTS * BACK), 1) == route * BACK + rank)
    for b in range(4):
        cols = slice(b * 512, b * 512 + 512)
        gin[:, cols] = dot(take, ret[:, cols]).astype(BF16)

    remote(tot.at[0, c], zb.at[0, 1 - c], zs_s.at[0], zs_r.at[0, 1 - c], sibling).wait_recv()
    for s in (1, 2, 3):
        for core in (0, 1):
            remote(tot.at[s, core], zb.at[s, core], zs_s.at[0], zs_r.at[s, core], sibling).wait_recv()
    for core in (0, 1):
        acc = zb[0, core].astype(F32) + zb[1, core].astype(F32)
        grads[core] = acc + (zb[2, core].astype(F32) + zb[3, core].astype(F32))

    for w in wz + sends + finals + backs + [dx_out]:
        w.wait_send()
    for i, (dx, rel) in enumerate(far + [(0, 0)]):
        to_sibling(i, dx, rel).wait_send()
    for way in (0, 1):
        for t in range(4):
            for q in (1, 2, 3):
                ag(way, t, q).wait_send()
            for s in range(4):
                rs(way, t, s).wait_send()


def body(tokens, cotangent, routes, expert_gates, gate_proj, up_proj, down_proj):
    vmem = pl.BlockSpec(memory_space=pltpu.VMEM)
    dma = pltpu.SemaphoreType.DMA
    gin, grads = pl.pallas_call(
        kernel,
        out_shape=(
            jax.ShapeDtypeStruct((TOK, D), BF16),
            jax.ShapeDtypeStruct((2, WROWS, 128), F32),
        ),
        in_specs=[vmem] * 7,
        out_specs=(vmem, vmem),
        scratch_shapes=[
            pltpu.VMEM((EXPERTS * SEND, D), BF16),
            pltpu.VMEM((4, NY, WROWS, BLK), BF16),
            pltpu.VMEM((2, EXPERTS * SEND, D), BF16),
            pltpu.VMEM((2 * ROWS, D), BF16),
            pltpu.VMEM((2 * ROWS, D), BF16),
            pltpu.VMEM((4, NY, WROWS, BLK), BF16),
            pltpu.VMEM((2, 4, 4, WROWS, BLK), BF16),
            pltpu.VMEM((4, 2, WROWS, 128), BF16),
            pltpu.VMEM((4, 2, WROWS, 128), BF16),
            pltpu.VMEM((2, EXPERTS * BACK, D), BF16),
            pltpu.VMEM((EXPERTS * BACK, D), BF16),
            pltpu.VMEM((EXPERTS * BACK, D), BF16),
            pltpu.VMEM((4 * GU, 2 * ROWS), BF16),
            dma((7,)), dma((7,)), dma, dma((8,)), dma((8,)), dma((3,)), dma((3,)),
            dma((2, 4, 3)), dma((2, 4, 3)), dma, dma, dma((7,)), dma((7,)),
            dma((2, 4, 4)), dma((2, 4, 4)), dma((7,)), dma((4, 2)),
        ],
        compiler_params=pltpu.CompilerParams(
            collective_id=0, has_side_effects=True, vmem_limit_bytes=56 * 2**20
        ),
    )(routes, expert_gates, tokens, cotangent, gate_proj, up_proj, down_proj)
    parts = jnp.concatenate([grads[0].reshape(3, HALF_HID, 128), grads[1].reshape(3, HALF_HID, 128)], axis=1)
    return gin, parts[0].T, parts[1].T, parts[2]


def solution(mesh):
    in_specs = (
        P(("dp", "expert"), None),
        P(("dp", "expert"), None),
        P(("dp", "expert"), None),
        P(("dp", "expert"), None),
        P(None, "expert"),
        P(None, "expert"),
        P("expert", None),
    )
    out_specs = (P(("dp", "expert"), None), P("dp", "expert"), P("dp", "expert"), P("expert", "dp"))
    return jax.shard_map(body, mesh=mesh, in_specs=in_specs, out_specs=out_specs, check_vma=False)
```

time: 395 us -> 132 us (0.33)
  waiting for transfers between devices: 291 us -> 0 us
  Pallas kernels: 0 us -> 122 us
  starting transfers between devices: 32.5 us -> 0 us
  local copies, waits for them, and re-layouts: 31.1 us -> 7.59 us
  matrix products: 16.3 us -> 0 us
  between operations: 14 us -> 0.66 us
  other arithmetic: 8.37 us -> 0.71 us
    unnamed x6 -> x0, waiting for transfers between devices: 155 us -> none
    all_to_all x3 -> x0, waiting for transfers between devices: 136 us -> none  [the longest x1 70.2 us: body(): lax.all_to_all(copies(dy_slots), 'expert', split_axis=0, concat_axis=0, t...]
    pallas_call x0 -> x1, Pallas kernels: none -> 122 us  [body(): pl.pallas_call(kernel, out_shape=(jax.ShapeDtypeStruct((TOK, D), BF16), j...]
    all_to_all x3 -> x0, starting transfers between devices: 32.2 us -> none  [the longest x1 14 us: body(): lax.all_to_all(copies(dy_slots), 'expert', split_axis=0, concat_axis=0, t...]
    dot_general x7 -> x0, matrix products: 16.3 us -> none  [the longest x1 4.36 us: body(): lax.dot_general(joined_grads, joined_proj, by_width, preferred_element_ty...]
    reshape x4 -> x0, local copies, waits for them, and re-layouts: 10.3 us -> none  [the longest x1 4.28 us: body(): partial_value.reshape(expert_devs, capacity, model_dim)]
    gather x3 -> x0, local copies, waits for them, and re-layouts: 4.6 us -> none  [the longest x1 2.67 us: body(): jnp.take(cotangent, slot_table, axis=0, mode='fill', fill_value=0)]
    broadcast_in_dim x4 -> x0, local copies, waits for them, and re-layouts: 4.49 us -> none  [copies(): jnp.broadcast_to(spread, (EXPERTS, group_size, capacity, model_dim))]
  transfers between devices with their start and end apart: 6 -> 0, of which waited for: 5 -> 0; matrix products, arithmetic and copies ran while one was open for 7% -> 0% of each run, Pallas kernels for 0% -> 0%
where the time goes in v1:
time: 132 us; the launch traced here: 131 us
  Pallas kernels  122 us (92%)
  local copies, waits for them, and re-layouts  7.59 us (6%)
    pallas_call x1, Pallas kernels, body(): pl.pallas_call(kernel, out_shape=(jax.ShapeDtypeStruct((TOK, D), BF16), j...  122 us
    unnamed x11, local copies, waits for them, and re-layouts  6.53 us

profile of v1, /device:TPU:1, one launch (start us, length us, event | category | flops | bytes accessed | tf_op | source)
XLA Modules:
  0.0 131.5 jit_solution(14716936294768720098)
XLA Ops:
  0.6 0.0 copy-start.2
  0.6 1.4 %copy.11.routes = s32[128,1]{1,0:T(8,128)} copy(s32[128,1]{0,1:T(1,128)} %param.9) | data formatting | bytes 1024 | tf_op args[2]
  2.0 0.0 copy-done.2
  2.0 0.7 copy.12.gates
  2.8 0.0 copy-start
  2.8 2.3 %copy.13.gp = bf16[2048,192]{1,0:T(8,128)(2,1)} copy(bf16[2048,192]{0,1:T(8,128)(2,1)} %param.11) | data formatting | bytes 1572864 | tf_op args[4]
  5.1 0.0 copy-done
  5.1 1.3 copy.14.up
  6.4 122.5 %shard_map.102 = (bf16[128,2048]{1,0:T(8,128)(2,1)}, f32[2,288,128]{2,1,0:T(8,128)}) custom-call(s32[128,1]{1,0:T(8,128)} %copy.11.routes, f32[128,1]{1,0:T(8,128)} %copy.12.gates, bf16[128,2048]{1,0:T(8,128)(2,1)} %tok.1, bf16[128,2048]{1,0:T(8,128)(2,1)} %cot.1, bf16[2048,192]{1,0:T(8,128)(2,1)} %copy.13.gp, bf16[2048,192]{1,0:T(8,128)(2,1)} %copy.14.up, ...), custom_call_target="tpu_custom_call" | custom-call | tf_op jit(solution)/shard_map/pallas_call | solution.py:328
  128.9 0.0 copy-start.1
  128.9 1.1 fusion.5
  129.9 0.7 fusion.4
  130.7 0.0 copy-done.1
  130.7 0.8 copy.16
Async XLA Ops:
  0.6 1.4 %copy-start.2 = (f32[128,1]{0,1:T(1,128)S(1)}, f32[128,1]{0,1:T(1,128)}, u32[]{:S(2)}) copy-start(f32[128,1]{0,1:T(1,128)} %param.10) | copy-start | bytes 1540
  2.8 2.3 %copy-start = (bf16[2048,192]{0,1:T(8,128)(2,1)S(1)}, bf16[2048,192]{0,1:T(8,128)(2,1)}, u32[]{:S(2)}) copy-start(bf16[2048,192]{0,1:T(8,128)(2,1)} %param.12) | copy-start | bytes 2359300
  128.9 1.8 %copy-start.1 = (bf16[128,2048]{1,0:T(8,128)(2,1)S(1)}, bf16[128,2048]{1,0:T(8,128)(2,1)}, u32[]{:S(2)}) copy-start(bf16[128,2048]{1,0:T(8,128)(2,1)} %get-tuple-element.17) | copy-start | bytes 1572868

commit v2 on v1

v2 whole, which is shorter than its diff:
```python
import jax
import jax.numpy as jnp
from jax import lax
from jax.experimental import pallas as pl
from jax.experimental.pallas import tpu as pltpu
from jax.sharding import PartitionSpec as P

MESH = pl.DeviceIdType.MESH
EXPERTS = 8
MOST = 18
TOK = 128
D = 2048
NX, NY, NZ = 4, 8, 8
HALF_HID = 96
WROWS = 3 * HALF_HID
GU = 2 * HALF_HID
BLK = D // NY
ROWS = EXPERTS * MOST
WIDE = 512
MSG = 144
F32 = jnp.float32
BF16 = jnp.bfloat16
NT = (((1,), (1,)), ((), ()))
TN = (((0,), (0,)), ((), ()))
NN = (((1,), (0,)), ((), ()))


def dot(a, b, dims=NN):
    return lax.dot_general(a, b, dims, preferred_element_type=F32)


def iota(shape, dim):
    return lax.broadcasted_iota(jnp.int32, shape, dim)


def pick(cond):
    return jnp.where(cond, 1.0, 0.0).astype(BF16)


def packed(ref, lead, start, size):
    parts = [ref[(*lead, slice(k * MSG + start, k * MSG + start + size))] for k in range(EXPERTS)]
    parts += [ref[(*lead, slice(k * MSG + 128, k * MSG + MSG))] for k in range(EXPERTS)]
    return jnp.concatenate(parts, axis=0)


def kernel(
    routes, gates, tok, cot, gp, up, dn, gin, g_out, u_out, d_out,
    xd, wall, rcv, xs, ds, gr, rb, tot, zb, dxp, dxr, dxn, ret, dgu, hid,
    own_s, disp_s, disp_r, loc, nb_s, nb_r, sib_s, sib_r, wz_s, wz_r, ag_s, ag_r,
    dx_s, dx_r, dn_s, dn_r, ret_s, ret_r, rs_s, rs_r, zs_s, zs_r,
):
    di, ei = lax.axis_index("dp"), lax.axis_index("expert")
    y, c = di // 2, di % 2
    x, z = ei // NZ, ei % NZ
    h, zl = z // 4, z % 4
    sibling = {"dp": y * 2 + (1 - c), "expert": ei}
    above = {"dp": ((y + 1) % NY) * 2 + c, "expert": ei}
    below = {"dp": ((y + NY - 1) % NY) * 2 + c, "expert": ei}
    beside = {"dp": di, "expert": x * NZ + z + 1 - 2 * (z % 2)}

    def at_x(dx, rel):
        return ((x + dx) % NX) * NZ + (z if rel == 0 else NZ - 1 - z)

    def mirror(core):
        return {"dp": y * 2 + core, "expert": x * NZ + h * 4 + 3 - zl}

    far = [(dx, 1) for dx in (0, 1, 3, 2)] + [(dx, 0) for dx in (1, 3, 2)]

    def remote(src, dst, send, recv, where):
        return pltpu.make_async_remote_copy(
            src_ref=src, dst_ref=dst, send_sem=send, recv_sem=recv,
            device_id=where, device_id_type=MESH,
        )

    barrier = pltpu.get_barrier_semaphore()
    partners = [sibling, above, below, beside, mirror(0), mirror(1)]
    partners += [{"dp": di, "expert": at_x(dx, rel)} for dx, rel in far]
    for p in partners:
        pl.semaphore_signal(barrier, inc=1, device_id=p, device_id_type=MESH)

    half_hid = pl.ds(pl.multiple_of(c * HALF_HID, HALF_HID), HALF_HID)

    def own_block(b):
        cols = pl.ds(pl.multiple_of(b * BLK, BLK), BLK)
        return [
            pltpu.make_async_copy(
                w.at[half_hid, cols], wall.at[0, b, pl.ds(m * HALF_HID, HALF_HID)], own_s.at[b, m]
            )
            for m, w in enumerate((gp, up, dn))
        ]

    for k in range(NY):
        for w in own_block((y + k) % NY):
            w.start()

    route = routes[...]
    one_hot = pick(iota((16, TOK), 0) == route)
    earlier = pick(iota((TOK, TOK), 0) < iota((TOK, TOK), 1))
    rank = jnp.sum(dot(one_hot, earlier) * one_hot.astype(F32), axis=0, keepdims=True)
    rank = rank.astype(jnp.int32)
    low = rank < 16
    slots = iota((EXPERTS * 32, TOK), 0)
    main = jnp.where(low, route * 32 + rank, -1)
    place = jnp.concatenate(
        [pick(slots == main), pick(slots == jnp.where(low, main + 16, -1))], axis=1
    )
    slots = iota((EXPERTS * 16, TOK), 0)
    diagonal = iota((TOK, TOK), 0) == iota((TOK, TOK), 1)
    weight = jnp.sum(jnp.where(diagonal, gates[...], 0.0), axis=1, keepdims=True)
    rest = jnp.zeros((EXPERTS * 16, WIDE), F32)
    for b in range(4):
        cols = slice(b * WIDE, b * WIDE + WIDE)
        scaled = (cot[:, cols].astype(F32) * weight).astype(BF16)
        both = jnp.concatenate([tok[:, cols], scaled], axis=0)
        out = dot(place, both).astype(BF16)
        over = jnp.where(low, -1, route * 16 + 4 * b + rank - 16)
        over = jnp.concatenate(
            [pick(slots == over), pick(slots == jnp.where(low, -1, over + 2))], axis=1
        )
        rest = rest + dot(over, both)
        for e in range(EXPERTS):
            xd[e * MSG + b * 32:e * MSG + b * 32 + 32] = out[e * 32:e * 32 + 32]
    rest = rest.astype(BF16)
    for e in range(EXPERTS):
        xd[e * MSG + 128:e * MSG + MSG] = rest[e * 16:e * 16 + 16]

    for w in own_block(y):
        w.wait()
    pl.semaphore_wait(barrier, len(partners))
    wz = remote(wall.at[0, y], wall.at[1, y], wz_s, wz_r, mirror(c))
    wz.start()

    def msg(e):
        return pl.ds(pl.multiple_of(e * MSG, MSG), MSG)

    sends = []
    for i, (dx, rel) in enumerate(far):
        e = ((x + dx) % NX) * 2 + (h if rel == 0 else 1 - h)
        sends.append(
            remote(
                xd.at[msg(e)], rcv.at[c, msg(x * 2 + rel)],
                disp_s.at[i], disp_r.at[i], {"dp": di, "expert": at_x(dx, rel)},
            )
        )
        sends[-1].start()
    keep = pltpu.make_async_copy(xd.at[msg(x * 2 + h)], rcv.at[c, msg(x * 2)], loc)
    keep.start()

    def slot(i):
        dx, rel = (far + [(0, 0)])[i]
        return msg(((x - dx + NX) % NX) * 2 + rel)

    def to_beside(i):
        return remote(
            rcv.at[c, slot(i)], rcv.at[2 + c, slot(i)], nb_s.at[i], nb_r.at[i], beside
        )

    def from_beside(i):
        return remote(rcv.at[c, slot(i)], rcv.at[2 + c, slot(i)], nb_s.at[i], nb_r.at[i], beside)

    def to_sibling(n, i):
        ref = rcv.at[2 * n + c, slot(i)]
        return remote(ref, ref, sib_s.at[n, i], sib_r.at[n, i], sibling)

    def from_sibling(n, i):
        ref = rcv.at[2 * n + 1 - c, slot(i)]
        return remote(ref, ref, sib_s.at[n, i], sib_r.at[n, i], sibling)

    def ag(way, t):
        b = (y - t + NY) % NY if way == 0 else (y + t) % NY
        ref = wall.at[1, b]
        if t == 3:
            ref = wall.at[1, b, pl.ds(way * (WROWS // 2), WROWS // 2)]
        return remote(ref, ref, ag_s.at[way, t], ag_r.at[way, t], above if way == 0 else below)

    def ag_in(way, t):
        b = (y - 1 - t + NY) % NY if way == 0 else (y + 1 + t) % NY
        ref = wall.at[1, b]
        if t == 3:
            ref = wall.at[1, b, pl.ds(way * (WROWS // 2), WROWS // 2)]
        remote(ref, ref, ag_s.at[way, t], ag_r.at[way, t], above if way == 0 else below).wait_recv()

    def ag_step(t):
        for way in (0, 1):
            ag_in(way, t - 1)
            ag(way, t).start()

    def forward(i):
        if i < 7:
            sends[i].wait_recv()
        else:
            keep.wait()
        to_beside(i).start()
        to_sibling(0, i).start()

    def forward_beside(i):
        from_beside(i).wait_recv()
        to_sibling(1, i).start()

    forward(7)
    wz.wait_recv()
    for way in (0, 1):
        ag(way, 0).start()
    for i in (4, 5, 6):
        forward(i)
    ag_step(1)
    for i in (0, 1):
        forward(i)
    ag_step(2)
    for i in (2, 3):
        forward(i)
    for i in (7, 4, 5, 6):
        forward_beside(i)
    ag_step(3)
    for k in range(1, NY):
        for w in own_block((y + k) % NY):
            w.wait()
    for i in (0, 1, 2, 3):
        forward_beside(i)

    row = iota((ROWS, 1), 0)
    source = jnp.zeros((ROWS, 1), jnp.int32)
    for m in range(1, EXPERTS):
        source = source + jnp.where(row >= MOST * m, 1, 0)
    row = row - MOST * source
    col = iota((ROWS, EXPERTS * 48), 1)

    def gather_rows(n, core):
        part = 2 * n + core
        at = slice(part * ROWS, part * ROWS + ROWS)
        for b in range(4):
            cols = slice(b * WIDE, b * WIDE + WIDE)
            sel_x = pick(col == jnp.where(row < 16, source * 32 + row, 240 + source * 16 + 4 * b + row))
            sel_d = pick(col == jnp.where(row < 16, source * 32 + 16 + row, 242 + source * 16 + 4 * b + row))
            rows = packed(rcv, (part,), b * 32, 32)
            xs[at, cols] = dot(sel_x, rows).astype(BF16)
            ds[at, cols] = dot(sel_d, rows).astype(BF16)

    for n in (0, 1):
        for i in range(8):
            from_sibling(n, i).wait_recv()
        for core in (0, 1):
            gather_rows(n, core)

    def rs(way, t, s):
        if t == 0:
            half = pl.ds(way * (WROWS // 2), WROWS // 2)
            src, dst = gr.at[s, (y + 4) % NY, half], rb.at[way, 0, s, half]
        else:
            src, dst = rb.at[way, t - 1, s], rb.at[way, t, s]
        return remote(
            src, dst, rs_s.at[way, t, s], rs_r.at[way, t, s], above if way == 0 else below
        )

    def activations(s):
        pre = jnp.zeros((GU, 4 * ROWS), F32)
        dh = jnp.zeros((HALF_HID, 4 * ROWS), F32)
        for b in range(NY):
            cols = slice(b * BLK, b * BLK + BLK)
            pre = pre + dot(wall[s, b, 0:GU, :], xs[:, cols], NT)
            dh = dh + dot(wall[s, b, GU:WROWS, :], ds[:, cols], NT)
        g, u = pre[0:HALF_HID], pre[HALF_HID:GU]
        sig = 1.0 / (1.0 + jnp.exp(-g))
        hid[s * HALF_HID:s * HALF_HID + HALF_HID] = (g * sig * u).astype(BF16)
        dgu[s * GU:s * GU + HALF_HID] = (dh * u * sig * (1.0 + g * (1.0 - sig))).astype(BF16)
        dgu[s * GU + HALF_HID:s * GU + GU] = (dh * g * sig).astype(BF16)

    def weight_grads(s):
        for b in range(NY):
            cols = slice(b * BLK, b * BLK + BLK)
            gr[s, b, 0:GU, :] = dot(dgu[s * GU:s * GU + GU], xs[:, cols]).astype(BF16)
            gr[s, b, GU:WROWS, :] = dot(hid[s * HALF_HID:s * HALF_HID + HALF_HID], ds[:, cols]).astype(BF16)
        for way in (0, 1):
            rs(way, 0, s).start()

    activations(0)
    weight_grads(0)
    for way in (0, 1):
        ag_in(way, 3)
    activations(1)

    j, i_ = iota((EXPERTS * 16, ROWS), 0), iota((EXPERTS * 16, ROWS), 1)
    spread = pick(i_ == j + 2 * (j // 16))
    lasts = [jnp.zeros((EXPERTS * 16, BLK), F32) for _ in range(4)]
    for b in range(NY):
        cols = slice(b * BLK, b * BLK + BLK)
        rhs = jnp.concatenate([wall[s, b, 0:GU, :] for s in (0, 1)], axis=0)
        dx = dot(dgu[...], rhs, TN).astype(BF16)
        own = j % 16 - 2 * b
        spread_last = pick((i_ == MOST * (j // 16) + 16 + own) & (own >= 0) & (own < 2))
        for part in range(4):
            mine = dx[part * ROWS:part * ROWS + ROWS]
            out = dot(spread, mine).astype(BF16)
            lasts[part] = lasts[part] + dot(spread_last, mine)
            for k in range(EXPERTS):
                dxp[part, k * MSG + b * 16:k * MSG + b * 16 + 16] = out[k * 16:k * 16 + 16]
    for part in range(4):
        last = lasts[part].astype(BF16)
        for k in range(EXPERTS):
            dxp[part, k * MSG + 128:k * MSG + MSG] = last[k * 16:k * 16 + 16]

    dx_out = [
        remote(dxp.at[2 * n + 1 - c], dxr.at[n], dx_s.at[n], dx_r.at[n], sibling) for n in (0, 1)
    ]
    for n in (1, 0):
        dx_out[n].start()
    weight_grads(1)

    def rs_add(way, t, s):
        rs(way, t, s).wait_recv()
        b = (y + 3 - t) % NY if way == 0 else (y - 3 + t + NY) % NY
        if t == 0:
            lo, hi = way * (WROWS // 2), (1 - way) * (WROWS // 2)
            a, o = pl.ds(lo, WROWS // 2), pl.ds(hi, WROWS // 2)
            rb[way, 0, s, a, :] = (rb[way, 0, s, a, :].astype(F32) + gr[s, b, a, :].astype(F32)).astype(BF16)
            rb[way, 0, s, o, :] = gr[s, b, o, :]
        else:
            rb[way, t, s] = (rb[way, t, s].astype(F32) + gr[s, b].astype(F32)).astype(BF16)

    def rs_step(t, s):
        for way in (0, 1):
            rs_add(way, t, s)
            rs(way, t + 1, s).start()

    dx_beside = remote(dxr.at[1], dxn, dn_s, dn_r, beside)
    dx_out[1].wait_recv()
    dxr[1] = (dxr[1].astype(F32) + dxp[2 + c].astype(F32)).astype(BF16)
    dx_beside.start()
    for s in (0, 1):
        rs_step(0, s)
    dx_out[0].wait_recv()
    for s in (0, 1):
        rs_step(1, s)
    dx_beside.wait_recv()
    dxr[0] = (dxr[0].astype(F32) + dxp[c].astype(F32) + dxn[...].astype(F32)).astype(BF16)
    backs = []
    for i, (dx, rel) in enumerate(far):
        backs.append(
            remote(
                dxr.at[0, msg(((x + dx) % NX) * 2 + rel)], ret.at[msg(x * 2 + h)],
                ret_s.at[i], ret_r.at[i], {"dp": di, "expert": at_x(dx, rel)},
            )
        )
        backs[-1].start()
    back_own = pltpu.make_async_copy(dxr.at[0, msg(x * 2)], ret.at[msg(x * 2 + h)], loc)
    back_own.start()
    for s in (1, 0):
        rs_step(2, s)

    finals = []
    for s in (1, 0):
        for way in (0, 1):
            rs(way, 3, s).wait_recv()
        total = gr[s, y].astype(F32) + rb[0, 3, s].astype(F32) + rb[1, 3, s].astype(F32)
        for core in (0, 1):
            tot[s, core] = total[:, core * 128:core * 128 + 128].astype(BF16)
        if s:
            for core in (0, 1):
                finals.append(
                    remote(tot.at[1, core], zb.at[1, c], zs_s.at[core], zs_r.at[1, c], mirror(core))
                )
                finals[-1].start()
        else:
            finals.append(remote(tot.at[0, 1 - c], zb.at[0, c], zs_s.at[2], zs_r.at[0, c], sibling))
            finals[-1].start()
            zb[0, c] = tot[0, c]

    back_own.wait()
    for b in backs:
        b.wait_recv()

    def column(row):
        held = jnp.sum(jnp.where(diagonal, row.astype(F32), 0.0), axis=1, keepdims=True)
        return held.astype(jnp.int32)

    route, rank = column(route), column(rank)
    cols_of = iota((TOK, EXPERTS * 32), 1)
    for b in range(NY):
        at = jnp.where(rank < 16, route * 16 + rank, 112 + route * 16 + 2 * b + rank)
        take = pick(cols_of == at)
        gin[:, b * BLK:b * BLK + BLK] = dot(take, packed(ret, (), b * 16, 16)).astype(BF16)

    remote(tot.at[0, c], zb.at[0, 1 - c], zs_s.at[0], zs_r.at[0, 1 - c], sibling).wait_recv()
    for core in (0, 1):
        remote(tot.at[1, core], zb.at[1, core], zs_s.at[0], zs_r.at[1, core], sibling).wait_recv()
    for core in (0, 1):
        acc = zb[0, core].astype(F32) + zb[1, core].astype(F32)
        for m, out in enumerate((g_out, u_out, d_out)):
            out[core * HALF_HID:(core + 1) * HALF_HID] = acc[m * HALF_HID:(m + 1) * HALF_HID]

    for w in [wz] + sends + finals + backs + dx_out + [dx_beside]:
        w.wait_send()
    for i in range(8):
        to_beside(i).wait_send()
        for n in (0, 1):
            to_sibling(n, i).wait_send()
    for way in (0, 1):
        for t in range(4):
            ag(way, t).wait_send()
            for s in (0, 1):
                rs(way, t, s).wait_send()


def body(tokens, cotangent, routes, expert_gates, gate_proj, up_proj, down_proj):
    vmem = pl.BlockSpec(memory_space=pltpu.VMEM)
    dma = pltpu.SemaphoreType.DMA
    anywhere = pl.BlockSpec(memory_space=pl.ANY)
    gin, g_t, u_t, d_g = pl.pallas_call(
        kernel,
        out_shape=(
            jax.ShapeDtypeStruct((TOK, D), BF16),
            jax.ShapeDtypeStruct((GU, 128), F32),
            jax.ShapeDtypeStruct((GU, 128), F32),
            jax.ShapeDtypeStruct((GU, 128), F32),
        ),
        in_specs=[vmem] * 4 + [anywhere] * 3,
        out_specs=(vmem,) * 4,
        scratch_shapes=[
            pltpu.VMEM((EXPERTS * MSG, WIDE), BF16),
            pltpu.VMEM((2, NY, WROWS, BLK), BF16),
            pltpu.VMEM((4, EXPERTS * MSG, WIDE), BF16),
            pltpu.VMEM((4 * ROWS, D), BF16),
            pltpu.VMEM((4 * ROWS, D), BF16),
            pltpu.VMEM((2, NY, WROWS, BLK), BF16),
            pltpu.VMEM((2, 4, 2, WROWS, BLK), BF16),
            pltpu.VMEM((2, 2, WROWS, 128), BF16),
            pltpu.VMEM((2, 2, WROWS, 128), BF16),
            pltpu.VMEM((4, EXPERTS * MSG, BLK), BF16),
            pltpu.VMEM((2, EXPERTS * MSG, BLK), BF16),
            pltpu.VMEM((EXPERTS * MSG, BLK), BF16),
            pltpu.VMEM((EXPERTS * MSG, BLK), BF16),
            pltpu.VMEM((2 * GU, 4 * ROWS), BF16),
            pltpu.VMEM((2 * HALF_HID, 4 * ROWS), BF16),
            dma((NY, 3)), dma((7,)), dma((7,)), dma, dma((8,)), dma((8,)), dma((2, 8)), dma((2, 8)),
            dma, dma, dma((2, 4)), dma((2, 4)), dma((2,)), dma((2,)), dma, dma,
            dma((7,)), dma((7,)), dma((2, 4, 2)), dma((2, 4, 2)), dma((3,)), dma((2, 2)),
        ],
        compiler_params=pltpu.CompilerParams(
            collective_id=0, has_side_effects=True, vmem_limit_bytes=56 * 2**20
        ),
    )(
        routes.reshape(1, TOK), expert_gates.reshape(1, TOK), tokens, cotangent,
        gate_proj.T, up_proj.T, down_proj,
    )
    return gin, g_t.T, u_t.T, d_g


def solution(mesh):
    in_specs = (
        P(("dp", "expert"), None),
        P(("dp", "expert"), None),
        P(("dp", "expert"), None),
        P(("dp", "expert"), None),
        P(None, "expert"),
        P(None, "expert"),
        P("expert", None),
    )
    out_specs = (P(("dp", "expert"), None), P("dp", "expert"), P("dp", "expert"), P("expert", "dp"))
    return jax.shard_map(body, mesh=mesh, in_specs=in_specs, out_specs=out_specs, check_vma=False)
```

time: 132 us -> 110 us (0.83)
  Pallas kernels: 122 us -> 105 us
  local copies, waits for them, and re-layouts: 7.59 us -> 4.42 us
    pallas_call x1, Pallas kernels: 122 us -> 105 us  [body(): pl.pallas_call(kernel, out_shape=(jax.ShapeDtypeStruct((TOK, D), BF16), j...]
    unnamed x11 -> x10, local copies, waits for them, and re-layouts: 6.53 us -> 4.42 us
where the time goes in v2:
time: 110 us
  Pallas kernels  105 us (95%)
  local copies, waits for them, and re-layouts  4.42 us (4%)
    pallas_call x1, Pallas kernels, body(): pl.pallas_call(kernel, out_shape=(jax.ShapeDtypeStruct((TOK, D), BF16), j...  105 us
    unnamed x10, local copies, waits for them, and re-layouts  4.42 us

profile of v2, /device:TPU:1, one launch (start us, length us, event | category | flops | bytes accessed | tf_op | source)
XLA Modules:
  0.0 109.9 jit_solution(14112800587735918863)
XLA Ops:
  0.6 104.9 %shard_map.102 = (bf16[128,2048]{1,0:T(8,128)(2,1)}, f32[192,128]{1,0:T(8,128)}, f32[192,128]{1,0:T(8,128)}, f32[192,128]{1,0:T(8,128)}) custom-call(s32[1,128]{1,0:T(1,128)} %bitcast.10, f32[1,128]{1,0:T(1,128)} %bitcast.11, bf16[128,2048]{1,0:T(8,128)(2,1)} %tok.1, bf16[128,2048]{1,0:T(8,128)(2,1)} %cot.1, bf16[192,2048]{1,0:T(8,128)(2,1)} %bitcast.6, ...), custom_call_target="tpu_custom_call" | custom-call | tf_op jit(solution)/shard_map/pallas_call | solution.py:408
  105.5 0.0 copy-start.2
  105.5 1.9 %copy.15 = bf16[128,2048]{1,0:T(8,128)(2,1)} copy(bf16[128,2048]{1,0:T(8,128)(2,1)} %get-tuple-element.16) | data formatting | bytes 1048576
  107.4 0.0 copy-done.2
  107.4 0.0 copy-start.1
  107.4 0.6 copy.16
  108.1 0.3 copy-done.1
  108.4 0.0 copy-start
  108.4 0.6 copy.17
  109.0 0.3 copy-done
  109.3 0.6 copy.18
Async XLA Ops:
  105.5 1.9 %copy-start.2 = (f32[192,128]{1,0:T(8,128)S(1)}, f32[192,128]{1,0:T(8,128)}, u32[]{:S(2)}) copy-start(f32[192,128]{1,0:T(8,128)} %get-tuple-element.9) | copy-start | bytes 294916
  107.4 0.9 copy-start.1
  108.4 0.9 copy-start

commit v3 on v2

--- a/solution.py
+++ b/solution.py
@@ -37,14 +37,14 @@
     return jnp.where(cond, 1.0, 0.0).astype(BF16)
 
 
-def packed(ref, lead, start, size):
-    parts = [ref[(*lead, slice(k * MSG + start, k * MSG + start + size))] for k in range(EXPERTS)]
-    parts += [ref[(*lead, slice(k * MSG + 128, k * MSG + MSG))] for k in range(EXPERTS)]
+def packed(messages, start, size):
+    parts = [ref[(*lead, slice(at + start, at + start + size))] for ref, lead, at in messages]
+    parts += [ref[(*lead, slice(at + 128, at + MSG))] for ref, lead, at in messages]
     return jnp.concatenate(parts, axis=0)
 
 
 def kernel(
-    routes, gates, tok, cot, gp, up, dn, gin, g_out, u_out, d_out,
+    routes, gates, tok, cot, gp, up, dn, gin, grads,
     xd, wall, rcv, xs, ds, gr, rb, tot, zb, dxp, dxr, dxn, ret, dgu, hid,
     own_s, disp_s, disp_r, loc, nb_s, nb_r, sib_s, sib_r, wz_s, wz_r, ag_s, ag_r,
     dx_s, dx_r, dn_s, dn_r, ret_s, ret_r, rs_s, rs_r, zs_s, zs_r,
@@ -64,7 +64,7 @@
     def mirror(core):
         return {"dp": y * 2 + core, "expert": x * NZ + h * 4 + 3 - zl}
 
-    far = [(dx, 1) for dx in (0, 1, 3, 2)] + [(dx, 0) for dx in (1, 3, 2)]
+    far = [(0, 1), (1, 0), (3, 0), (2, 0), (1, 1), (3, 1), (2, 1)]
 
     def remote(src, dst, send, recv, where):
         return pltpu.make_async_remote_copy(
@@ -197,27 +197,6 @@
         from_beside(i).wait_recv()
         to_sibling(1, i).start()
 
-    forward(7)
-    wz.wait_recv()
-    for way in (0, 1):
-        ag(way, 0).start()
-    for i in (4, 5, 6):
-        forward(i)
-    ag_step(1)
-    for i in (0, 1):
-        forward(i)
-    ag_step(2)
-    for i in (2, 3):
-        forward(i)
-    for i in (7, 4, 5, 6):
-        forward_beside(i)
-    ag_step(3)
-    for k in range(1, NY):
-        for w in own_block((y + k) % NY):
-            w.wait()
-    for i in (0, 1, 2, 3):
-        forward_beside(i)
-
     row = iota((ROWS, 1), 0)
     source = jnp.zeros((ROWS, 1), jnp.int32)
     for m in range(1, EXPERTS):
@@ -225,22 +204,89 @@
     row = row - MOST * source
     col = iota((ROWS, EXPERTS * 48), 1)
 
-    def gather_rows(n, core):
-        part = 2 * n + core
-        at = slice(part * ROWS, part * ROWS + ROWS)
+    def gather_rows(g, n):
+        for i in ((0, 4, 5, 6) if g else (7, 1, 2, 3)):
+            from_sibling(n, i).wait_recv()
+        at = slice((2 * g + n) * ROWS, (2 * g + n) * ROWS + ROWS)
+        messages = [(rcv, (2 * n + k // 4,), (2 * (k % 4) + g) * MSG) for k in range(EXPERTS)]
         for b in range(4):
             cols = slice(b * WIDE, b * WIDE + WIDE)
             sel_x = pick(col == jnp.where(row < 16, source * 32 + row, 240 + source * 16 + 4 * b + row))
             sel_d = pick(col == jnp.where(row < 16, source * 32 + 16 + row, 242 + source * 16 + 4 * b + row))
-            rows = packed(rcv, (part,), b * 32, 32)
+            rows = packed(messages, b * 32, 32)
             xs[at, cols] = dot(sel_x, rows).astype(BF16)
             ds[at, cols] = dot(sel_d, rows).astype(BF16)
 
-    for n in (0, 1):
-        for i in range(8):
-            from_sibling(n, i).wait_recv()
-        for core in (0, 1):
-            gather_rows(n, core)
+    def group(g):
+        return slice(g * 2 * ROWS, (g + 1) * 2 * ROWS)
+
+    def activations(g, s):
+        pre = jnp.zeros((GU, 2 * ROWS), F32)
+        dh = jnp.zeros((HALF_HID, 2 * ROWS), F32)
+        for b in range(NY):
+            cols = slice(b * BLK, b * BLK + BLK)
+            pre = pre + dot(wall[s, b, 0:GU, :], xs[group(g), cols], NT)
+            dh = dh + dot(wall[s, b, GU:WROWS, :], ds[group(g), cols], NT)
+        gate, u = pre[0:HALF_HID], pre[HALF_HID:GU]
+        sig = 1.0 / (1.0 + jnp.exp(-gate))
+        hid[g, s * HALF_HID:s * HALF_HID + HALF_HID] = (gate * sig * u).astype(BF16)
+        dgu[g, s * GU:s * GU + HALF_HID] = (dh * u * sig * (1.0 + gate * (1.0 - sig))).astype(BF16)
+        dgu[g, s * GU + HALF_HID:s * GU + GU] = (dh * gate * sig).astype(BF16)
+
+    j, i_ = iota((EXPERTS * 16, ROWS), 0), iota((EXPERTS * 16, ROWS), 1)
+    spread = pick(i_ == j + 2 * (j // 16))
+
+    def dx_out(g, n):
+        return remote(dxp.at[g, 2 * n + 1 - c], dxr.at[g, n], dx_s.at[g, n], dx_r.at[g, n], sibling)
+
+    def input_grads(g):
+        lasts = [jnp.zeros((EXPERTS * 16, BLK), F32) for _ in range(2)]
+        for b in range(NY):
+            cols = slice(b * BLK, b * BLK + BLK)
+            rhs = jnp.concatenate([wall[s, b, 0:GU, :] for s in (0, 1)], axis=0)
+            dx = dot(dgu[g], rhs, TN).astype(BF16)
+            own = j % 16 - 2 * b
+            spread_last = pick((i_ == MOST * (j // 16) + 16 + own) & (own >= 0) & (own < 2))
+            for n in (0, 1):
+                mine = dx[n * ROWS:n * ROWS + ROWS]
+                out = dot(spread, mine).astype(BF16)
+                lasts[n] = lasts[n] + dot(spread_last, mine)
+                for k in range(EXPERTS):
+                    at = (k % 4) * MSG + b * 16
+                    dxp[g, 2 * n + k // 4, at:at + 16] = out[k * 16:k * 16 + 16]
+        for n in (1, 0):
+            last = lasts[n].astype(BF16)
+            for k in range(EXPERTS):
+                at = (k % 4) * MSG + 128
+                dxp[g, 2 * n + k // 4, at:at + 16] = last[k * 16:k * 16 + 16]
+            dx_out(g, n).start()
+
+    def dx_beside(g):
+        return remote(dxr.at[g, 1], dxn.at[g], dn_s.at[g], dn_r.at[g], beside)
+
+    def sum_for_beside(g):
+        dx_out(g, 1).wait_recv()
+        dxr[g, 1] = (dxr[g, 1].astype(F32) + dxp[g, 2 + c].astype(F32)).astype(BF16)
+        dx_beside(g).start()
+
+    backs = []
+    back_own = pltpu.make_async_copy(dxr.at[0, 0, msg(x)], ret.at[msg(x * 2 + h)], loc)
+
+    def send_back(g):
+        dx_out(g, 0).wait_recv()
+        dx_beside(g).wait_recv()
+        dxr[g, 0] = (dxr[g, 0].astype(F32) + dxp[g, c].astype(F32) + dxn[g].astype(F32)).astype(BF16)
+        for i, (dx, rel) in enumerate(far):
+            if rel == g:
+                backs.append(
+                    remote(
+                        dxr.at[g, 0, msg((x + dx) % NX)], ret.at[msg(x * 2 + h)],
+                        ret_s.at[i], ret_r.at[i], {"dp": di, "expert": at_x(dx, rel)},
+                    )
+                )
+                backs[-1].start()
+        if g == 0:
+            back_own.start()
 
     def rs(way, t, s):
         if t == 0:
@@ -252,59 +298,19 @@
             src, dst, rs_s.at[way, t, s], rs_r.at[way, t, s], above if way == 0 else below
         )
 
-    def activations(s):
-        pre = jnp.zeros((GU, 4 * ROWS), F32)
-        dh = jnp.zeros((HALF_HID, 4 * ROWS), F32)
-        for b in range(NY):
-            cols = slice(b * BLK, b * BLK + BLK)
-            pre = pre + dot(wall[s, b, 0:GU, :], xs[:, cols], NT)
-            dh = dh + dot(wall[s, b, GU:WROWS, :], ds[:, cols], NT)
-        g, u = pre[0:HALF_HID], pre[HALF_HID:GU]
-        sig = 1.0 / (1.0 + jnp.exp(-g))
-        hid[s * HALF_HID:s * HALF_HID + HALF_HID] = (g * sig * u).astype(BF16)
-        dgu[s * GU:s * GU + HALF_HID] = (dh * u * sig * (1.0 + g * (1.0 - sig))).astype(BF16)
-        dgu[s * GU + HALF_HID:s * GU + GU] = (dh * g * sig).astype(BF16)
-
-    def weight_grads(s):
-        for b in range(NY):
-            cols = slice(b * BLK, b * BLK + BLK)
-            gr[s, b, 0:GU, :] = dot(dgu[s * GU:s * GU + GU], xs[:, cols]).astype(BF16)
-            gr[s, b, GU:WROWS, :] = dot(hid[s * HALF_HID:s * HALF_HID + HALF_HID], ds[:, cols]).astype(BF16)
-        for way in (0, 1):
-            rs(way, 0, s).start()
-
-    activations(0)
-    weight_grads(0)
-    for way in (0, 1):
-        ag_in(way, 3)
-    activations(1)
-
-    j, i_ = iota((EXPERTS * 16, ROWS), 0), iota((EXPERTS * 16, ROWS), 1)
-    spread = pick(i_ == j + 2 * (j // 16))
-    lasts = [jnp.zeros((EXPERTS * 16, BLK), F32) for _ in range(4)]
-    for b in range(NY):
-        cols = slice(b * BLK, b * BLK + BLK)
-        rhs = jnp.concatenate([wall[s, b, 0:GU, :] for s in (0, 1)], axis=0)
-        dx = dot(dgu[...], rhs, TN).astype(BF16)
-        own = j % 16 - 2 * b
-        spread_last = pick((i_ == MOST * (j // 16) + 16 + own) & (own >= 0) & (own < 2))
-        for part in range(4):
-            mine = dx[part * ROWS:part * ROWS + ROWS]
-            out = dot(spread, mine).astype(BF16)
-            lasts[part] = lasts[part] + dot(spread_last, mine)
-            for k in range(EXPERTS):
-                dxp[part, k * MSG + b * 16:k * MSG + b * 16 + 16] = out[k * 16:k * 16 + 16]
-    for part in range(4):
-        last = lasts[part].astype(BF16)
-        for k in range(EXPERTS):
-            dxp[part, k * MSG + 128:k * MSG + MSG] = last[k * 16:k * 16 + 16]
-
-    dx_out = [
-        remote(dxp.at[2 * n + 1 - c], dxr.at[n], dx_s.at[n], dx_r.at[n], sibling) for n in (0, 1)
-    ]
-    for n in (1, 0):
-        dx_out[n].start()
-    weight_grads(1)
+    def weight_grads(s, b):
+        cols = pl.ds(pl.multiple_of(b * BLK, BLK), BLK)
+        gu, dn_ = jnp.zeros((GU, BLK), F32), jnp.zeros((HALF_HID, BLK), F32)
+        for g in (0, 1):
+            gu = gu + dot(dgu[g, s * GU:s * GU + GU], xs[group(g), cols])
+            dn_ = dn_ + dot(hid[g, s * HALF_HID:s * HALF_HID + HALF_HID], ds[group(g), cols])
+        gr[s, b, 0:GU, :] = gu.astype(BF16)
+        gr[s, b, GU:WROWS, :] = dn_.astype(BF16)
+
+    def grads_at(distance):
+        for s in (1, 0):
+            for b in sorted({distance, (NY - distance) % NY}):
+                weight_grads(s, (y + b) % NY)
 
     def rs_add(way, t, s):
         rs(way, t, s).wait_recv()
@@ -317,35 +323,60 @@
         else:
             rb[way, t, s] = (rb[way, t, s].astype(F32) + gr[s, b].astype(F32)).astype(BF16)
 
-    def rs_step(t, s):
+    def rs_step(t):
+        for s in (1, 0):
+            for way in (0, 1):
+                rs_add(way, t, s)
+                rs(way, t + 1, s).start()
+
+    forward(7)
+    wz.wait_recv()
+    for way in (0, 1):
+        ag(way, 0).start()
+    for i in (1, 2, 0, 3):
+        forward(i)
+    ag_step(1)
+    for i in (7, 1, 2, 3):
+        forward_beside(i)
+    forward(4)
+    ag_step(2)
+    gather_rows(0, 0)
+    forward(5)
+    gather_rows(0, 1)
+    ag_step(3)
+    for k in range(1, NY):
+        for w in own_block((y + k) % NY):
+            w.wait()
+    forward(6)
+    forward_beside(0)
+    activations(0, 0)
+    forward_beside(4)
+    for way in (0, 1):
+        ag_in(way, 3)
+    activations(0, 1)
+    forward_beside(5)
+    input_grads(0)
+    forward_beside(6)
+    gather_rows(1, 0)
+    gather_rows(1, 1)
+    activations(1, 1)
+    activations(1, 0)
+    for s in (1, 0):
+        weight_grads(s, (y + 4) % NY)
         for way in (0, 1):
-            rs_add(way, t, s)
-            rs(way, t + 1, s).start()
-
-    dx_beside = remote(dxr.at[1], dxn, dn_s, dn_r, beside)
-    dx_out[1].wait_recv()
-    dxr[1] = (dxr[1].astype(F32) + dxp[2 + c].astype(F32)).astype(BF16)
-    dx_beside.start()
-    for s in (0, 1):
-        rs_step(0, s)
-    dx_out[0].wait_recv()
-    for s in (0, 1):
-        rs_step(1, s)
-    dx_beside.wait_recv()
-    dxr[0] = (dxr[0].astype(F32) + dxp[c].astype(F32) + dxn[...].astype(F32)).astype(BF16)
-    backs = []
-    for i, (dx, rel) in enumerate(far):
-        backs.append(
-            remote(
-                dxr.at[0, msg(((x + dx) % NX) * 2 + rel)], ret.at[msg(x * 2 + h)],
-                ret_s.at[i], ret_r.at[i], {"dp": di, "expert": at_x(dx, rel)},
-            )
-        )
-        backs[-1].start()
-    back_own = pltpu.make_async_copy(dxr.at[0, msg(x * 2)], ret.at[msg(x * 2 + h)], loc)
-    back_own.start()
-    for s in (1, 0):
-        rs_step(2, s)
+            rs(way, 0, s).start()
+    sum_for_beside(0)
+    input_grads(1)
+    grads_at(3)
+    sum_for_beside(1)
+    rs_step(0)
+    send_back(0)
+    grads_at(2)
+    rs_step(1)
+    send_back(1)
+    grads_at(1)
+    rs_step(2)
+    grads_at(0)
 
     finals = []
     for s in (1, 0):
@@ -378,18 +409,23 @@
     for b in range(NY):
         at = jnp.where(rank < 16, route * 16 + rank, 112 + route * 16 + 2 * b + rank)
         take = pick(cols_of == at)
-        gin[:, b * BLK:b * BLK + BLK] = dot(take, packed(ret, (), b * 16, 16)).astype(BF16)
+        rows = packed([(ret, (), k * MSG) for k in range(EXPERTS)], b * 16, 16)
+        gin[:, b * BLK:b * BLK + BLK] = dot(take, rows).astype(BF16)
 
     remote(tot.at[0, c], zb.at[0, 1 - c], zs_s.at[0], zs_r.at[0, 1 - c], sibling).wait_recv()
     for core in (0, 1):
         remote(tot.at[1, core], zb.at[1, core], zs_s.at[0], zs_r.at[1, core], sibling).wait_recv()
     for core in (0, 1):
         acc = zb[0, core].astype(F32) + zb[1, core].astype(F32)
-        for m, out in enumerate((g_out, u_out, d_out)):
-            out[core * HALF_HID:(core + 1) * HALF_HID] = acc[m * HALF_HID:(m + 1) * HALF_HID]
-
-    for w in [wz] + sends + finals + backs + dx_out + [dx_beside]:
+        for m in range(3):
+            grads[m, core * HALF_HID:(core + 1) * HALF_HID] = acc[m * HALF_HID:(m + 1) * HALF_HID]
+
+    for w in [wz] + sends + finals + backs:
         w.wait_send()
+    for g in (0, 1):
+        dx_beside(g).wait_send()
+        for n in (0, 1):
+            dx_out(g, n).wait_send()
     for i in range(8):
         to_beside(i).wait_send()
         for n in (0, 1):
@@ -405,16 +441,14 @@
     vmem = pl.BlockSpec(memory_space=pltpu.VMEM)
     dma = pltpu.SemaphoreType.DMA
     anywhere = pl.BlockSpec(memory_space=pl.ANY)
-    gin, g_t, u_t, d_g = pl.pallas_call(
+    gin, grads = pl.pallas_call(
         kernel,
         out_shape=(
             jax.ShapeDtypeStruct((TOK, D), BF16),
-            jax.ShapeDtypeStruct((GU, 128), F32),
-            jax.ShapeDtypeStruct((GU, 128), F32),
-            jax.ShapeDtypeStruct((GU, 128), F32),
+            jax.ShapeDtypeStruct((3, GU, 128), F32),
         ),
         in_specs=[vmem] * 4 + [anywhere] * 3,
-        out_specs=(vmem,) * 4,
+        out_specs=(vmem, vmem),
         scratch_shapes=[
             pltpu.VMEM((EXPERTS * MSG, WIDE), BF16),
             pltpu.VMEM((2, NY, WROWS, BLK), BF16),
@@ -425,14 +459,14 @@
             pltpu.VMEM((2, 4, 2, WROWS, BLK), BF16),
             pltpu.VMEM((2, 2, WROWS, 128), BF16),
             pltpu.VMEM((2, 2, WROWS, 128), BF16),
-            pltpu.VMEM((4, EXPERTS * MSG, BLK), BF16),
-            pltpu.VMEM((2, EXPERTS * MSG, BLK), BF16),
+            pltpu.VMEM((2, 4, NX * MSG, BLK), BF16),
+            pltpu.VMEM((2, 2, NX * MSG, BLK), BF16),
+            pltpu.VMEM((2, NX * MSG, BLK), BF16),
             pltpu.VMEM((EXPERTS * MSG, BLK), BF16),
-            pltpu.VMEM((EXPERTS * MSG, BLK), BF16),
-            pltpu.VMEM((2 * GU, 4 * ROWS), BF16),
-            pltpu.VMEM((2 * HALF_HID, 4 * ROWS), BF16),
+            pltpu.VMEM((2, 2 * GU, 2 * ROWS), BF16),
+            pltpu.VMEM((2, 2 * HALF_HID, 2 * ROWS), BF16),
             dma((NY, 3)), dma((7,)), dma((7,)), dma, dma((8,)), dma((8,)), dma((2, 8)), dma((2, 8)),
-            dma, dma, dma((2, 4)), dma((2, 4)), dma((2,)), dma((2,)), dma, dma,
+            dma, dma, dma((2, 4)), dma((2, 4)), dma((2, 2)), dma((2, 2)), dma((2,)), dma((2,)),
             dma((7,)), dma((7,)), dma((2, 4, 2)), dma((2, 4, 2)), dma((3,)), dma((2, 2)),
         ],
         compiler_params=pltpu.CompilerParams(
@@ -442,7 +476,7 @@
         routes.reshape(1, TOK), expert_gates.reshape(1, TOK), tokens, cotangent,
         gate_proj.T, up_proj.T, down_proj,
     )
-    return gin, g_t.T, u_t.T, d_g
+    return gin, grads[0].T, grads[1].T, grads[2]
 
 
 def solution(mesh):

time: 110 us -> 102 us (0.927)
  Pallas kernels: 105 us -> 98.7 us
  local copies, waits for them, and re-layouts: 4.42 us -> 2.55 us
    pallas_call x1, Pallas kernels: 105 us -> 98.7 us  [body(): pl.pallas_call(kernel, out_shape=(jax.ShapeDtypeStruct((TOK, D), BF16), j...]
    unnamed x10 -> x3, local copies, waits for them, and re-layouts: 4.42 us -> 0.8 us
    squeeze x0 -> x1, local copies, waits for them, and re-layouts: none -> 1.76 us  [body(): return (gin, grads[0].T, grads[1].T, grads[2])]
where the time goes in v3:
time: 102 us
  Pallas kernels  98.7 us (97%)
  local copies, waits for them, and re-layouts  2.55 us (2%)
    pallas_call x1, Pallas kernels, body(): pl.pallas_call(kernel, out_shape=(jax.ShapeDtypeStruct((TOK, D), BF16), j...  98.7 us

profile of v3, /device:TPU:1, one launch (start us, length us, event | category | flops | bytes accessed | tf_op | source)
XLA Modules:
  0.0 101.9 jit_solution(17777084931937974163)
XLA Ops:
  0.6 98.7 %shard_map.102 = (bf16[128,2048]{1,0:T(8,128)(2,1)}, f32[3,192,128]{2,1,0:T(8,128)}) custom-call(s32[1,128]{1,0:T(1,128)} %bitcast.16, f32[1,128]{1,0:T(1,128)} %bitcast.17, bf16[128,2048]{1,0:T(8,128)(2,1)} %tok.1, bf16[128,2048]{1,0:T(8,128)(2,1)} %cot.1, bf16[192,2048]{1,0:T(8,128)(2,1)} %bitcast.14, bf16[192,2048]{1,0:T(8,128)(2,1)} %bitcast.15, ...), custom_call_target="tpu_custom_call" | custom-call | tf_op jit(solution)/shard_map/pallas_call | solution.py:444
  99.3 0.0 copy-start
  99.3 1.8 %slice_bitcast_fusion = (f32[192,128]{1,0:T(8,128)}, f32[128,192]{0,1:T(8,128)}, f32[128,192]{0,1:T(8,128)}) fusion(f32[3,192,128]{2,1,0:T(8,128)} %get-tuple-element.7), kind=kLoop, calls=%fused_computation | loop fusion | bytes 589824 | tf_op jit(solution)/shard_map/squeeze | solution.py:479
  101.1 0.0 copy-done
  101.1 0.8 copy.12
Async XLA Ops:
  99.3 1.8 %copy-start = (bf16[128,2048]{1,0:T(8,128)(2,1)S(1)}, bf16[128,2048]{1,0:T(8,128)(2,1)}, u32[]{:S(2)}) copy-start(bf16[128,2048]{1,0:T(8,128)(2,1)} %get-tuple-element.15) | copy-start | bytes 1572868

commit v4 on v3

--- a/solution.py
+++ b/solution.py
@@ -217,21 +217,21 @@
             xs[at, cols] = dot(sel_x, rows).astype(BF16)
             ds[at, cols] = dot(sel_d, rows).astype(BF16)
 
-    def group(g):
-        return slice(g * 2 * ROWS, (g + 1) * 2 * ROWS)
-
-    def activations(g, s):
-        pre = jnp.zeros((GU, 2 * ROWS), F32)
-        dh = jnp.zeros((HALF_HID, 2 * ROWS), F32)
+    def part(p):
+        return slice(p * ROWS, p * ROWS + ROWS)
+
+    def activations(p, s):
+        pre = jnp.zeros((GU, ROWS), F32)
+        dh = jnp.zeros((HALF_HID, ROWS), F32)
         for b in range(NY):
             cols = slice(b * BLK, b * BLK + BLK)
-            pre = pre + dot(wall[s, b, 0:GU, :], xs[group(g), cols], NT)
-            dh = dh + dot(wall[s, b, GU:WROWS, :], ds[group(g), cols], NT)
+            pre = pre + dot(wall[s, b, 0:GU, :], xs[part(p), cols], NT)
+            dh = dh + dot(wall[s, b, GU:WROWS, :], ds[part(p), cols], NT)
         gate, u = pre[0:HALF_HID], pre[HALF_HID:GU]
         sig = 1.0 / (1.0 + jnp.exp(-gate))
-        hid[g, s * HALF_HID:s * HALF_HID + HALF_HID] = (gate * sig * u).astype(BF16)
-        dgu[g, s * GU:s * GU + HALF_HID] = (dh * u * sig * (1.0 + gate * (1.0 - sig))).astype(BF16)
-        dgu[g, s * GU + HALF_HID:s * GU + GU] = (dh * gate * sig).astype(BF16)
+        hid[p, s * HALF_HID:s * HALF_HID + HALF_HID] = (gate * sig * u).astype(BF16)
+        dgu[p, s * GU:s * GU + HALF_HID] = (dh * u * sig * (1.0 + gate * (1.0 - sig))).astype(BF16)
+        dgu[p, s * GU + HALF_HID:s * GU + GU] = (dh * gate * sig).astype(BF16)
 
     j, i_ = iota((EXPERTS * 16, ROWS), 0), iota((EXPERTS * 16, ROWS), 1)
     spread = pick(i_ == j + 2 * (j // 16))
@@ -239,54 +239,55 @@
     def dx_out(g, n):
         return remote(dxp.at[g, 2 * n + 1 - c], dxr.at[g, n], dx_s.at[g, n], dx_r.at[g, n], sibling)
 
-    def input_grads(g):
-        lasts = [jnp.zeros((EXPERTS * 16, BLK), F32) for _ in range(2)]
+    def input_grads(g, n):
+        last = jnp.zeros((EXPERTS * 16, BLK), F32)
         for b in range(NY):
             cols = slice(b * BLK, b * BLK + BLK)
             rhs = jnp.concatenate([wall[s, b, 0:GU, :] for s in (0, 1)], axis=0)
-            dx = dot(dgu[g], rhs, TN).astype(BF16)
+            dx = dot(dgu[2 * g + n], rhs, TN).astype(BF16)
             own = j % 16 - 2 * b
             spread_last = pick((i_ == MOST * (j // 16) + 16 + own) & (own >= 0) & (own < 2))
-            for n in (0, 1):
-                mine = dx[n * ROWS:n * ROWS + ROWS]
-                out = dot(spread, mine).astype(BF16)
-                lasts[n] = lasts[n] + dot(spread_last, mine)
-                for k in range(EXPERTS):
-                    at = (k % 4) * MSG + b * 16
-                    dxp[g, 2 * n + k // 4, at:at + 16] = out[k * 16:k * 16 + 16]
-        for n in (1, 0):
-            last = lasts[n].astype(BF16)
+            out = dot(spread, dx).astype(BF16)
+            last = last + dot(spread_last, dx)
             for k in range(EXPERTS):
-                at = (k % 4) * MSG + 128
-                dxp[g, 2 * n + k // 4, at:at + 16] = last[k * 16:k * 16 + 16]
-            dx_out(g, n).start()
-
-    def dx_beside(g):
-        return remote(dxr.at[g, 1], dxn.at[g], dn_s.at[g], dn_r.at[g], beside)
+                at = (k % 4) * MSG + b * 16
+                dxp[g, 2 * n + k // 4, at:at + 16] = out[k * 16:k * 16 + 16]
+        last = last.astype(BF16)
+        for k in range(EXPERTS):
+            at = (k % 4) * MSG + 128
+            dxp[g, 2 * n + k // 4, at:at + 16] = last[k * 16:k * 16 + 16]
+        dx_out(g, n).start()
+
+    def dx_beside(g, dx):
+        at = msg((x + dx) % NX)
+        return remote(dxr.at[g, 1, at], dxn.at[g, at], dn_s.at[g, dx], dn_r.at[g, dx], beside)
 
     def sum_for_beside(g):
         dx_out(g, 1).wait_recv()
-        dxr[g, 1] = (dxr[g, 1].astype(F32) + dxp[g, 2 + c].astype(F32)).astype(BF16)
-        dx_beside(g).start()
+        for dx in (0, 1, 3, 2):
+            at = msg((x + dx) % NX)
+            dxr[g, 1, at] = (dxr[g, 1, at].astype(F32) + dxp[g, 2 + c, at].astype(F32)).astype(BF16)
+            dx_beside(g, dx).start()
 
     backs = []
     back_own = pltpu.make_async_copy(dxr.at[0, 0, msg(x)], ret.at[msg(x * 2 + h)], loc)
 
-    def send_back(g):
-        dx_out(g, 0).wait_recv()
-        dx_beside(g).wait_recv()
-        dxr[g, 0] = (dxr[g, 0].astype(F32) + dxp[g, c].astype(F32) + dxn[g].astype(F32)).astype(BF16)
-        for i, (dx, rel) in enumerate(far):
-            if rel == g:
-                backs.append(
-                    remote(
-                        dxr.at[g, 0, msg((x + dx) % NX)], ret.at[msg(x * 2 + h)],
-                        ret_s.at[i], ret_r.at[i], {"dp": di, "expert": at_x(dx, rel)},
-                    )
-                )
-                backs[-1].start()
-        if g == 0:
+    def send_back(g, dx):
+        at = msg((x + dx) % NX)
+        dx_beside(g, dx).wait_recv()
+        total = dxr[g, 0, at].astype(F32) + dxp[g, c, at].astype(F32) + dxn[g, at].astype(F32)
+        dxr[g, 0, at] = total.astype(BF16)
+        if (dx, g) == (0, 0):
             back_own.start()
+            return
+        i = far.index((dx, g))
+        backs.append(
+            remote(
+                dxr.at[g, 0, at], ret.at[msg(x * 2 + h)],
+                ret_s.at[i], ret_r.at[i], {"dp": di, "expert": at_x(dx, g)},
+            )
+        )
+        backs[-1].start()
 
     def rs(way, t, s):
         if t == 0:
@@ -301,9 +302,9 @@
     def weight_grads(s, b):
         cols = pl.ds(pl.multiple_of(b * BLK, BLK), BLK)
         gu, dn_ = jnp.zeros((GU, BLK), F32), jnp.zeros((HALF_HID, BLK), F32)
-        for g in (0, 1):
-            gu = gu + dot(dgu[g, s * GU:s * GU + GU], xs[group(g), cols])
-            dn_ = dn_ + dot(hid[g, s * HALF_HID:s * HALF_HID + HALF_HID], ds[group(g), cols])
+        for p in range(4):
+            gu = gu + dot(dgu[p, s * GU:s * GU + GU], xs[part(p), cols])
+            dn_ = dn_ + dot(hid[p, s * HALF_HID:s * HALF_HID + HALF_HID], ds[part(p), cols])
         gr[s, b, 0:GU, :] = gu.astype(BF16)
         gr[s, b, GU:WROWS, :] = dn_.astype(BF16)
 
@@ -333,47 +334,54 @@
     wz.wait_recv()
     for way in (0, 1):
         ag(way, 0).start()
-    for i in (1, 2, 0, 3):
+    for i in (1, 2, 3, 0):
         forward(i)
     ag_step(1)
+    forward(4)
+    ag_step(2)
+    forward(5)
+    ag_step(3)
+    forward(6)
     for i in (7, 1, 2, 3):
         forward_beside(i)
-    forward(4)
-    ag_step(2)
-    gather_rows(0, 0)
-    forward(5)
-    gather_rows(0, 1)
-    ag_step(3)
     for k in range(1, NY):
         for w in own_block((y + k) % NY):
             w.wait()
-    forward(6)
-    forward_beside(0)
-    activations(0, 0)
-    forward_beside(4)
+    for n in (0, 1):
+        gather_rows(0, n)
+        activations(n, 0)
     for way in (0, 1):
         ag_in(way, 3)
-    activations(0, 1)
-    forward_beside(5)
-    input_grads(0)
-    forward_beside(6)
+    for n in (1, 0):
+        activations(n, 1)
+        input_grads(0, n)
     gather_rows(1, 0)
+    activations(2, 0)
+    activations(2, 1)
+    for i in (0, 4, 5, 6):
+        forward_beside(i)
+    sum_for_beside(0)
     gather_rows(1, 1)
-    activations(1, 1)
-    activations(1, 0)
     for s in (1, 0):
+        activations(3, s)
         weight_grads(s, (y + 4) % NY)
         for way in (0, 1):
             rs(way, 0, s).start()
-    sum_for_beside(0)
-    input_grads(1)
+    input_grads(1, 1)
+    sum_for_beside(1)
+    input_grads(1, 0)
     grads_at(3)
-    sum_for_beside(1)
+    dx_out(0, 0).wait_recv()
     rs_step(0)
-    send_back(0)
+    for dx in (0, 1, 3, 2):
+        send_back(0, dx)
+    dx_out(1, 0).wait_recv()
+    for dx in (0, 1):
+        send_back(1, dx)
     grads_at(2)
+    for dx in (3, 2):
+        send_back(1, dx)
     rs_step(1)
-    send_back(1)
     grads_at(1)
     rs_step(2)
     grads_at(0)
@@ -423,7 +431,8 @@
     for w in [wz] + sends + finals + backs:
         w.wait_send()
     for g in (0, 1):
-        dx_beside(g).wait_send()
+        for dx in range(NX):
+            dx_beside(g, dx).wait_send()
         for n in (0, 1):
             dx_out(g, n).wait_send()
     for i in range(8):
@@ -463,10 +472,10 @@
             pltpu.VMEM((2, 2, NX * MSG, BLK), BF16),
             pltpu.VMEM((2, NX * MSG, BLK), BF16),
             pltpu.VMEM((EXPERTS * MSG, BLK), BF16),
-            pltpu.VMEM((2, 2 * GU, 2 * ROWS), BF16),
-            pltpu.VMEM((2, 2 * HALF_HID, 2 * ROWS), BF16),
+            pltpu.VMEM((4, 2 * GU, ROWS), BF16),
+            pltpu.VMEM((4, 2 * HALF_HID, ROWS), BF16),
             dma((NY, 3)), dma((7,)), dma((7,)), dma, dma((8,)), dma((8,)), dma((2, 8)), dma((2, 8)),
-            dma, dma, dma((2, 4)), dma((2, 4)), dma((2, 2)), dma((2, 2)), dma((2,)), dma((2,)),
+            dma, dma, dma((2, 4)), dma((2, 4)), dma((2, 2)), dma((2, 2)), dma((2, NX)), dma((2, NX)),
             dma((7,)), dma((7,)), dma((2, 4, 2)), dma((2, 4, 2)), dma((3,)), dma((2, 2)),
         ],
         compiler_params=pltpu.CompilerParams(

time: 102 us -> 97.2 us (0.953)
  Pallas kernels: 98.7 us -> 93.8 us
    pallas_call x1, Pallas kernels: 98.7 us -> 93.8 us  [body(): pl.pallas_call(kernel, out_shape=(jax.ShapeDtypeStruct((TOK, D), BF16), j...]
where the time goes in v4:
time: 97.2 us; the launch traced here: 97 us
  Pallas kernels  93.8 us (97%)
  local copies, waits for them, and re-layouts  2.55 us (3%)
    pallas_call x1, Pallas kernels, body(): pl.pallas_call(kernel, out_shape=(jax.ShapeDtypeStruct((TOK, D), BF16), j...  93.8 us

profile of v4, /device:TPU:1, one launch (start us, length us, event | category | flops | bytes accessed | tf_op | source)
XLA Modules:
  0.0 97.0 jit_solution(8121861697112632079)
XLA Ops:
  0.6 93.8 %shard_map.102 = (bf16[128,2048]{1,0:T(8,128)(2,1)}, f32[3,192,128]{2,1,0:T(8,128)}) custom-call(s32[1,128]{1,0:T(1,128)} %bitcast.16, f32[1,128]{1,0:T(1,128)} %bitcast.17, bf16[128,2048]{1,0:T(8,128)(2,1)} %tok.1, bf16[128,2048]{1,0:T(8,128)(2,1)} %cot.1, bf16[192,2048]{1,0:T(8,128)(2,1)} %bitcast.14, bf16[192,2048]{1,0:T(8,128)(2,1)} %bitcast.15, ...), custom_call_target="tpu_custom_call" | custom-call | tf_op jit(solution)/shard_map/pallas_call | solution.py:453
  94.4 0.0 copy-start
  94.4 1.8 %slice_bitcast_fusion = (f32[192,128]{1,0:T(8,128)}, f32[128,192]{0,1:T(8,128)}, f32[128,192]{0,1:T(8,128)}) fusion(f32[3,192,128]{2,1,0:T(8,128)} %get-tuple-element.7), kind=kLoop, calls=%fused_computation | loop fusion | bytes 589824 | tf_op jit(solution)/shard_map/squeeze | solution.py:488
  96.2 0.0 copy-done
  96.2 0.8 copy.12
Async XLA Ops:
  94.4 1.8 %copy-start = (bf16[128,2048]{1,0:T(8,128)(2,1)S(1)}, bf16[128,2048]{1,0:T(8,128)(2,1)}, u32[]{:S(2)}) copy-start(bf16[128,2048]{1,0:T(8,128)(2,1)} %get-tuple-element.15) | copy-start | bytes 1572868

commit v5 on v4

--- a/solution.py
+++ b/solution.py
@@ -44,11 +44,17 @@
 
 
 def kernel(
-    routes, gates, tok, cot, gp, up, dn, gin, grads,
-    xd, wall, rcv, xs, ds, gr, rb, tot, zb, dxp, dxr, dxn, ret, dgu, hid,
-    own_s, disp_s, disp_r, loc, nb_s, nb_r, sib_s, sib_r, wz_s, wz_r, ag_s, ag_r,
+    routes, gates, tok_in, cot_in, gp, up, dn, gin_out, grads,
+    xd, wall, rcv, xs, ds, gr, rb, tot, zb, dxp, dxr, dxn, ret, dgu, hid, tok, cot, gin,
+    io_s, own_s, disp_s, disp_r, loc, nb_s, nb_r, sib_s, sib_r, wz_s, wz_r, ag_s, ag_r,
     dx_s, dx_r, dn_s, dn_r, ret_s, ret_r, rs_s, rs_r, zs_s, zs_r,
 ):
+    loads = [
+        pltpu.make_async_copy(src, dst, io_s.at[k])
+        for k, (src, dst) in enumerate(((tok_in, tok), (cot_in, cot)))
+    ]
+    for w in loads:
+        w.start()
     di, ei = lax.axis_index("dp"), lax.axis_index("expert")
     y, c = di // 2, di % 2
     x, z = ei // NZ, ei % NZ
@@ -89,9 +95,8 @@
             for m, w in enumerate((gp, up, dn))
         ]
 
-    for k in range(NY):
-        for w in own_block((y + k) % NY):
-            w.start()
+    for w in own_block(y):
+        w.start()
 
     route = routes[...]
     one_hot = pick(iota((16, TOK), 0) == route)
@@ -108,6 +113,8 @@
     diagonal = iota((TOK, TOK), 0) == iota((TOK, TOK), 1)
     weight = jnp.sum(jnp.where(diagonal, gates[...], 0.0), axis=1, keepdims=True)
     rest = jnp.zeros((EXPERTS * 16, WIDE), F32)
+    for w in loads:
+        w.wait()
     for b in range(4):
         cols = slice(b * WIDE, b * WIDE + WIDE)
         scaled = (cot[:, cols].astype(F32) * weight).astype(BF16)
@@ -145,6 +152,9 @@
         sends[-1].start()
     keep = pltpu.make_async_copy(xd.at[msg(x * 2 + h)], rcv.at[c, msg(x * 2)], loc)
     keep.start()
+    for k in range(1, NY):
+        for w in own_block((y + k) % NY):
+            w.start()
 
     def slot(i):
         dx, rel = (far + [(0, 0)])[i]
@@ -386,6 +396,24 @@
     rs_step(2)
     grads_at(0)
 
+    for w in [wz] + sends:
+        w.wait_send()
+    for g in (0, 1):
+        for dx in range(NX):
+            dx_beside(g, dx).wait_send()
+        for n in (0, 1):
+            dx_out(g, n).wait_send()
+    for i in range(8):
+        to_beside(i).wait_send()
+        for n in (0, 1):
+            to_sibling(n, i).wait_send()
+    for way in (0, 1):
+        for t in range(4):
+            ag(way, t).wait_send()
+        for t in range(3):
+            for s in (0, 1):
+                rs(way, t, s).wait_send()
+
     finals = []
     for s in (1, 0):
         for way in (0, 1):
@@ -419,6 +447,8 @@
         take = pick(cols_of == at)
         rows = packed([(ret, (), k * MSG) for k in range(EXPERTS)], b * 16, 16)
         gin[:, b * BLK:b * BLK + BLK] = dot(take, rows).astype(BF16)
+    store = pltpu.make_async_copy(gin, gin_out, io_s.at[2])
+    store.start()
 
     remote(tot.at[0, c], zb.at[0, 1 - c], zs_s.at[0], zs_r.at[0, 1 - c], sibling).wait_recv()
     for core in (0, 1):
@@ -428,22 +458,12 @@
         for m in range(3):
             grads[m, core * HALF_HID:(core + 1) * HALF_HID] = acc[m * HALF_HID:(m + 1) * HALF_HID]
 
-    for w in [wz] + sends + finals + backs:
+    store.wait()
+    for w in finals + backs:
         w.wait_send()
-    for g in (0, 1):
-        for dx in range(NX):
-            dx_beside(g, dx).wait_send()
-        for n in (0, 1):
-            dx_out(g, n).wait_send()
-    for i in range(8):
-        to_beside(i).wait_send()
-        for n in (0, 1):
-            to_sibling(n, i).wait_send()
     for way in (0, 1):
-        for t in range(4):
-            ag(way, t).wait_send()
-            for s in (0, 1):
-                rs(way, t, s).wait_send()
+        for s in (0, 1):
+            rs(way, 3, s).wait_send()
 
 
 def body(tokens, cotangent, routes, expert_gates, gate_proj, up_proj, down_proj):
@@ -456,8 +476,8 @@
             jax.ShapeDtypeStruct((TOK, D), BF16),
             jax.ShapeDtypeStruct((3, GU, 128), F32),
         ),
-        in_specs=[vmem] * 4 + [anywhere] * 3,
-        out_specs=(vmem, vmem),
+        in_specs=[vmem] * 2 + [anywhere] * 5,
+        out_specs=(anywhere, vmem),
         scratch_shapes=[
             pltpu.VMEM((EXPERTS * MSG, WIDE), BF16),
             pltpu.VMEM((2, NY, WROWS, BLK), BF16),
@@ -474,6 +494,10 @@
             pltpu.VMEM((EXPERTS * MSG, BLK), BF16),
             pltpu.VMEM((4, 2 * GU, ROWS), BF16),
             pltpu.VMEM((4, 2 * HALF_HID, ROWS), BF16),
+            pltpu.VMEM((TOK, D), BF16),
+            pltpu.VMEM((TOK, D), BF16),
+            pltpu.VMEM((TOK, D), BF16),
+            dma((3,)),
             dma((NY, 3)), dma((7,)), dma((7,)), dma, dma((8,)), dma((8,)), dma((2, 8)), dma((2, 8)),
             dma, dma, dma((2, 4)), dma((2, 4)), dma((2, 2)), dma((2, 2)), dma((2, NX)), dma((2, NX)),
             dma((7,)), dma((7,)), dma((2, 4, 2)), dma((2, 4, 2)), dma((3,)), dma((2, 2)),

time: 97.2 us -> 96.3 us (level)
  no operation moved by 1% of the time
where the time goes in v5:
time: 96.3 us; the launch traced here: 96.1 us
  Pallas kernels  92.9 us (96%)
  local copies, waits for them, and re-layouts  2.55 us (3%)
    pallas_call x1, Pallas kernels, body(): pl.pallas_call(kernel, out_shape=(jax.ShapeDtypeStruct((TOK, D), BF16), j...  92.9 us

profile of v5, /device:TPU:1, one launch (start us, length us, event | category | flops | bytes accessed | tf_op | source)
XLA Modules:
  0.0 96.1 jit_solution(16145856636516127148)
XLA Ops:
  0.6 92.9 %shard_map.102 = (bf16[128,2048]{1,0:T(8,128)(2,1)}, f32[3,192,128]{2,1,0:T(8,128)}) custom-call(s32[1,128]{1,0:T(1,128)} %bitcast.16, f32[1,128]{1,0:T(1,128)} %bitcast.17, bf16[128,2048]{1,0:T(8,128)(2,1)} %tok_in.1, bf16[128,2048]{1,0:T(8,128)(2,1)} %cot_in.1, bf16[192,2048]{1,0:T(8,128)(2,1)} %bitcast.14, bf16[192,2048]{1,0:T(8,128)(2,1)} %bitcast.15, ...), custom_call_target="tpu_custom_call" | custom-call | tf_op jit(solution)/shard_map/pallas_call | solution.py:473
  93.5 0.0 copy-start
  93.6 1.8 %slice_bitcast_fusion = (f32[192,128]{1,0:T(8,128)}, f32[128,192]{0,1:T(8,128)}, f32[128,192]{0,1:T(8,128)}) fusion(f32[3,192,128]{2,1,0:T(8,128)} %get-tuple-element.7), kind=kLoop, calls=%fused_computation | loop fusion | bytes 589824 | tf_op jit(solution)/shard_map/squeeze | solution.py:512
  95.3 0.0 copy-done
  95.3 0.8 copy.12
Async XLA Ops:
  93.5 1.8 %copy-start = (bf16[128,2048]{1,0:T(8,128)(2,1)S(1)}, bf16[128,2048]{1,0:T(8,128)(2,1)}, u32[]{:S(2)}) copy-start(bf16[128,2048]{1,0:T(8,128)(2,1)} %get-tuple-element.15) | copy-start | bytes 1572868
